TPU v7x, 256 devices: a whole 4x4x8 slice. The times are simulated.
256 devices in a mesh: pair: 64 (over z, y, core), aux: 4 (over x).
Axes of the slice: x: 4, y: 4, z: 8, core: 2. Of those that a mesh axis runs over, the one named last changes fastest.
Arguments:
- blocks: bfloat16 [4096, 512, 128], P('pair', 'aux'), may hold values from -1.5 to 1.5
- pno_coef: bfloat16 [1024, 512, 128], P('pair'), may hold values from -0.25 to 0.25
- source_dev: int32 [1024, 8], replicated, may hold values from 0 to 63, all different within a row; in each aligned block of 16 rows (0 to 15, 16 to 31, ...) at most 3 rows name the same one
- block_pos: int32 [1024, 8], replicated, may hold values from 0 to 63
- pno_energy: float32 [1024, 128], P('pair'), may hold values from 0.2 to 2
- occ_energy: float32 [1024], P('pair'), may hold values from 0.3 to 1.2
- pno_count: int32 [1024], P('pair'), may hold values from 32 to 128
- neighbour: int32 [1024, 4], P('pair'), may hold values from 0 to 1023, as said below
- coupling: float32 [1024, 4], P('pair'), may hold values from -1 to 1
- intersection: float32 [1024, 4, 128, 128], P('pair'), may hold values from -0.5 to 0.5
Outputs:
- amplitudes: float32 [1024, 128, 128], P('pair')
- pair_energy: float32 [1024], P('pair')
Inputs may be any that keep to these rules, and one draw needn't show every extreme that they name: `source_dev`: the 8 entries of a row are distinct. Within the rows of one index of pair (aligned blocks of 16 rows) no value appears more than 3 times, and in every draw some value appears exactly 3 times in some such block. neighbour[p, n] differs from p by 1 to 16; both ends of that reach occur in every draw.
All inputs are finite; a program needn't handle non-finite values.
Results may differ from a plain program's by a relative error of at most 0.0041.
Values may be sent and summed in bfloat16 or wider, within the bound.
A program may use at most 64 MiB of HBM per device.

v0:
```python
import jax
import jax.numpy as jnp
from jax import lax
from jax.sharding import PartitionSpec as P

ITERS = 3


HIGH = lax.Precision.HIGHEST


def with_halo(cells, sides, width):
    for axis, dim in sides:
        count = lax.axis_size(axis)
        ends = count - 1
        head = lax.slice_in_dim(cells, 0, width, axis=dim)
        tail = lax.slice_in_dim(cells, cells.shape[dim] - width, cells.shape[dim], axis=dim)
        cells = jnp.concatenate(
            [
                lax.ppermute(tail, axis, [(i, (i + 1) % count) for i in range(ends)]),
                cells,
                lax.ppermute(head, axis, [((i + 1) % count, i) for i in range(ends)]),
            ],
            axis=dim,
        )
    return cells


def neighbour_window(current):
    return with_halo(current, (("pair", 0),), current.shape[0])


def couple_rows(window, near_index, weights, intersections):
    near = window[near_index]
    first = jnp.einsum("gnab,gnbc->gnac", intersections, near, precision=HIGH)
    second = jnp.einsum("gnac,gndc->gnad", first, intersections, precision=HIGH)
    return jnp.einsum("gn,gnad->gad", weights, second, precision=HIGH)


def energies(integrals, current):
    return jnp.sum(integrals * (2.0 * current - jnp.swapaxes(current, 1, 2)), axis=(1, 2))


def shards(
    blocks,
    pno_coef,
    source_dev,
    block_pos,
    pno_energy,
    occ_energy,
    pno_count,
    neighbour,
    coupling,
    intersection,
):
    owners = lax.axis_size("pair")
    device = lax.axis_index("pair")
    pair_count = pno_coef.shape[0]
    requests = source_dev.shape[1]
    domain_tiles = requests // 2
    aux_width = blocks.shape[1]
    tile_width = blocks.shape[2]
    pno_width = pno_coef.shape[2]
    capacity = min(pair_count, max(2, 3 * domain_tiles * pair_count // owners))
    total_requests = pair_count * requests
    every_source = source_dev.reshape(owners, total_requests)
    every_position = block_pos.reshape(owners, total_requests)
    wanted = (every_source == device).astype(jnp.int32)
    ranking = jnp.cumsum(wanted, axis=1) - 1
    slot_ids = jnp.arange(capacity, dtype=jnp.int32)
    chosen = (wanted[:, None, :] == 1) & (ranking[:, None, :] == slot_ids[None, :, None])
    local_index = jnp.sum(jnp.where(chosen, every_position[:, None, :], 0), axis=2)
    outgoing = blocks[local_index]
    incoming = lax.all_to_all(outgoing, "pair", split_axis=0, concat_axis=0, tiled=True)
    own_source = lax.dynamic_index_in_dim(every_source, device, 0, keepdims=False)
    ordering = jnp.arange(total_requests, dtype=jnp.int32)
    earlier = (own_source[None, :] == own_source[:, None]) & (ordering[None, :] < ordering[:, None])
    own_rank = jnp.sum(earlier.astype(jnp.int32), axis=1)
    arrived = incoming.reshape(owners * capacity, aux_width, tile_width)[
        own_source * capacity + own_rank
    ]
    arrived = arrived.reshape(pair_count, 2, domain_tiles, aux_width, tile_width)
    coefs = pno_coef.reshape(pair_count, domain_tiles, tile_width, pno_width)
    projected = jnp.einsum(
        "qmtxp,qtpn->qmxn", arrived, coefs, preferred_element_type=jnp.float32
    ).astype(jnp.bfloat16)
    partial_ints = jnp.einsum(
        "qxa,qxb->qab", projected[:, 0], projected[:, 1], preferred_element_type=jnp.float32
    )
    positions = jnp.arange(pno_width, dtype=jnp.int32)
    live = (positions[None, :] < pno_count[:, None]).astype(jnp.float32)
    mask = live[:, :, None] * live[:, None, :]
    denom = pno_energy[:, :, None] + pno_energy[:, None, :] + occ_energy[:, None, None]
    window_base = (device - 1) * pair_count
    near_index = neighbour - window_base
    integrals = mask * lax.psum(partial_ints, "aux")
    amplitudes = -integrals / denom
    for sweep in range(ITERS):
        coupled = couple_rows(neighbour_window(amplitudes), near_index, coupling, intersection)
        amplitudes = mask * (coupled - integrals) / denom
    pair_energy = energies(integrals, amplitudes)
    return (amplitudes, pair_energy)


def solution(mesh):
    return jax.shard_map(
        shards,
        mesh=mesh,
        in_specs=(
            P("pair", "aux", None),
            P("pair", None, None),
            P(),
            P(),
            P("pair", None),
            P("pair"),
            P("pair"),
            P("pair", None),
            P("pair", None),
            P("pair", None, None, None),
        ),
        out_specs=(P("pair", None, None), P("pair")),
        check_vma=False,
    )
```

profile of v0, /device:TPU:25, one launch (start us, length us, event | category | flops | bytes accessed | tf_op | source)
XLA Modules:
  0.0 400.7 jit_solution(15429364380280814111)
XLA Ops:
  10.5 8.1 %gather_fusion = bf16[192,128,128]{2,1,0:T(8,128)(2,1)} fusion(bf16[64,128,128]{2,1,0:T(8,128)(2,1)S(1)} %copy-done, s32[1024]{0:T(1024)S(1)} %pad_clamp_fusion.2), kind=kCustom, calls=%fused_computation | custom fusion | bytes 12583680 | tf_op jit(solution)/shard_map/gather | solution.py:73
  18.6 12.4 %all-to-all-start = ((bf16[64,3,128,128]{3,2,1,0:T(8,128)(2,1)}), bf16[64,3,128,128]{3,2,1,0:T(8,128)(2,1)}, u32[]{:S(2)}, u32[]{:S(2)}) async-start(bf16[64,3,128,128]{3,2,1,0:T(8,128)(2,1)} %bitcast.54), calls=%async_computation | async-start | bytes 12582912 | tf_op jit(solution)/shard_map/all_to_all | solution.py:74
  31.2 138.5 %all-to-all-done = bf16[64,3,128,128]{3,2,1,0:T(8,128)(2,1)} async-done(((bf16[64,3,128,128]{3,2,1,0:T(8,128)(2,1)}), bf16[64,3,128,128]{3,2,1,0:T(8,128)(2,1)}, u32[]{:S(2)}, u32[]{:S(2)}) %all-to-all-start) | async-done | bytes 6291488 | tf_op jit(solution)/shard_map/all_to_all | solution.py:74
  169.7 5.9 %gather_fusion.1 = bf16[128,128,128]{2,1,0:T(8,128)(2,1)} fusion(bf16[192,128,128]{2,1,0:T(8,128)(2,1)} %bitcast.2, s32[1024]{0:T(1024)S(1)} %pad_clamp_fusion.1), kind=kCustom, calls=%fused_computation.1 | custom fusion | bytes 8389120 | tf_op jit(solution)/shard_map/gather | solution.py:79
  175.6 4.1 %bitcast_convert_fusion = bf16[16,2,128,128]{3,2,1,0:T(8,128)(2,1)S(1)} fusion(bf16[16,2,4,128,128]{4,3,2,1,0:T(8,128)(2,1)} %bitcast.58, bf16[16,4,128,128,1]{3,2,1,4,0:T(8,128)(2,1)} %bitcast.59), kind=kOutput, calls=%fused_computation.11 | convolution fusion | flops 537395200 | bytes 7340032 | tf_op jit(solution)/shard_map/qmtxp,qtpn->qmxn/dot_general | solution.py:84
  181.9 47.4 %all-reduce.2.cloned.1.call-done = f32[16,128,128]{2,1,0:T(8,128)} async-done(((f32[16,128,128]{2,1,0:T(8,128)}), f32[16,128,128]{2,1,0:T(8,128)}) %all-reduce.2.cloned.1.call-update) | async-done | bytes 1048592 | tf_op jit(solution)/shard_map/psum | solution.py:96
  231.4 5.1 %collective-permute-start = (f32[16,128,128]{1,2,0:T(8,128)S(1)}, f32[16,128,128]{1,2,0:T(8,128)}, u32[]{:S(2)}, u32[]{:S(2)}) collective-permute-start(f32[16,128,128]{1,2,0:T(8,128)S(1)} %fusion.5), channel_id=1, source_target_pairs={{0,4},{4,8},{8,12},{12,16},{16,20},{20,24},{24,28},{28,32},{32,36}... | collective-permute-start | bytes 3145736 | tf_op jit(solution)/shard_map/ppermute | solution.py:20
  236.5 2.1 collective-permute-start.1
  238.9 9.3 %collective-permute-done = f32[16,128,128]{1,2,0:T(8,128)} collective-permute-done((f32[16,128,128]{1,2,0:T(8,128)S(1)}, f32[16,128,128]{1,2,0:T(8,128)}, u32[]{:S(2)}, u32[]{:S(2)}) %collective-permute-start) | collective-permute-done | bytes 1048608 | tf_op jit(solution)/shard_map/ppermute | solution.py:20
  248.2 6.6 %collective-permute-done.1 = f32[16,128,128]{1,2,0:T(8,128)} collective-permute-done((f32[16,128,128]{1,2,0:T(8,128)S(1)}, f32[16,128,128]{1,2,0:T(8,128)}, u32[]{:S(2)}, u32[]{:S(2)}) %collective-permute-start.1) | collective-permute-done | bytes 1048608 | tf_op jit(solution)/shard_map/ppermute | solution.py:22
  254.8 3.6 pad_maximum_fusion
  258.4 4.6 %gather_fusion.2 = f32[64,128,128]{1,2,0:T(8,128)} fusion(f32[48,128,128]{1,2,0:T(8,128)} %pad_maximum_fusion, s32[1024]{0:T(1024)S(1)} %pad_clamp_fusion), kind=kCustom, calls=%fused_computation.2 | custom fusion | bytes 8388864 | tf_op jit(solution)/shard_map/gather | solution.py:34
  263.0 12.0 %fusion.13 = f32[16,4,128,128]{2,3,1,0:T(8,128)S(1)} fusion(f32[16,4,128,128]{2,3,1,0:T(8,128)} %bitcast.56, f32[16,4,128,128]{3,2,1,0:T(8,128)} %param.19), kind=kOutput, calls=%fused_computation.49 | convolution fusion | flops 1610612736 | bytes 12582912 | tf_op jit(solution)/shard_map/gnab,gnbc->gnac/dot_general | solution.py:35
  275.0 9.1 %multiply_reduce_fusion.2 = f32[16,128,128]{2,1,0:T(8,128)S(1)} fusion(f32[16,4,128,128]{2,3,1,0:T(8,128)S(1)} %fusion.13, f32[16,4,128,128]{3,2,1,0:T(8,128)S(1)} %copy-done.2, f32[16,4]{1,0:T(8,128)S(1)} %copy.68), kind=kOutput, calls=%fused_computation.7 | convolution fusion | flops 1612447744 | bytes 9437440 | tf_op jit(solution)/shard_map/gnac,gndc->gnad/dot_general | solution.py:36
  287.1 2.6 collective-permute-start.3
  289.7 9.1 %collective-permute-done.2 = f32[16,128,128]{1,2,0:T(8,128)S(1)} collective-permute-done((f32[16,128,128]{1,2,0:T(8,128)S(1)}, f32[16,128,128]{1,2,0:T(8,128)S(1)}, u32[]{:S(2)}, u32[]{:S(2)}) %collective-permute-start.2) | collective-permute-done | bytes 1048608 | tf_op jit(solution)/shard_map/ppermute | solution.py:20
  298.8 6.5 %collective-permute-done.3 = f32[16,128,128]{1,2,0:T(8,128)S(1)} collective-permute-done((f32[16,128,128]{1,2,0:T(8,128)S(1)}, f32[16,128,128]{1,2,0:T(8,128)S(1)}, u32[]{:S(2)}, u32[]{:S(2)}) %collective-permute-start.3) | collective-permute-done | bytes 1048608 | tf_op jit(solution)/shard_map/ppermute | solution.py:22
  305.3 2.0 pad_maximum_fusion.1
  307.4 4.6 %gather_fusion.3 = f32[64,128,128]{1,2,0:T(8,128)} fusion(f32[48,128,128]{1,2,0:T(8,128)} %pad_maximum_fusion.1, s32[1024]{0:T(1024)S(1)} %pad_clamp_fusion), kind=kCustom, calls=%fused_computation.3 | custom fusion | bytes 8388864 | tf_op jit(solution)/shard_map/gather | solution.py:34
  312.0 12.0 %fusion.14 = f32[16,4,128,128]{2,3,1,0:T(8,128)S(1)} fusion(f32[16,4,128,128]{2,3,1,0:T(8,128)} %bitcast.57, f32[16,4,128,128]{3,2,1,0:T(8,128)} %param.19), kind=kOutput, calls=%fused_computation.50 | convolution fusion | flops 1610612736 | bytes 12582912 | tf_op jit(solution)/shard_map/gnab,gnbc->gnac/dot_general | solution.py:35
  324.0 9.1 %multiply_reduce_fusion.1 = f32[16,128,128]{2,1,0:T(8,128)S(1)} fusion(f32[16,4,128,128]{2,3,1,0:T(8,128)S(1)} %fusion.14, f32[16,4,128,128]{3,2,1,0:T(8,128)S(1)} %copy-done.3, f32[16,4]{1,0:T(8,128)S(1)} %copy.68), kind=kOutput, calls=%fused_computation.6 | convolution fusion | flops 1612447744 | bytes 9437440 | tf_op jit(solution)/shard_map/gnac,gndc->gnad/dot_general | solution.py:36
  336.1 2.7 collective-permute-start.5
  338.8 9.0 %collective-permute-done.4 = f32[16,128,128]{1,2,0:T(8,128)S(1)} collective-permute-done((f32[16,128,128]{1,2,0:T(8,128)S(1)}, f32[16,128,128]{1,2,0:T(8,128)S(1)}, u32[]{:S(2)}, u32[]{:S(2)}) %collective-permute-start.4) | collective-permute-done | bytes 1048608 | tf_op jit(solution)/shard_map/ppermute | solution.py:20
  347.8 6.5 %collective-permute-done.5 = f32[16,128,128]{1,2,0:T(8,128)S(1)} collective-permute-done((f32[16,128,128]{1,2,0:T(8,128)S(1)}, f32[16,128,128]{1,2,0:T(8,128)S(1)}, u32[]{:S(2)}, u32[]{:S(2)}) %collective-permute-start.5) | collective-permute-done | bytes 1048608 | tf_op jit(solution)/shard_map/ppermute | solution.py:22
  354.3 2.0 pad_maximum_fusion.2
  356.4 4.6 %gather_fusion.4 = f32[64,128,128]{1,2,0:T(8,128)} fusion(f32[48,128,128]{1,2,0:T(8,128)} %pad_maximum_fusion.2, s32[1024]{0:T(1024)S(1)} %pad_clamp_fusion), kind=kCustom, calls=%fused_computation.4 | custom fusion | bytes 8388864 | tf_op jit(solution)/shard_map/gather | solution.py:34
  361.0 12.0 %fusion.15 = f32[16,4,128,128]{2,3,1,0:T(8,128)S(1)} fusion(f32[16,4,128,128]{2,3,1,0:T(8,128)} %bitcast.55, f32[16,4,128,128]{3,2,1,0:T(8,128)} %param.19), kind=kOutput, calls=%fused_computation.51 | convolution fusion | flops 1610612736 | bytes 12582912 | tf_op jit(solution)/shard_map/gnab,gnbc->gnac/dot_general | solution.py:35
  373.1 9.1 %multiply_reduce_fusion = f32[16,128,128]{2,1,0:T(8,128)S(1)} fusion(f32[16,4,128,128]{2,3,1,0:T(8,128)S(1)} %fusion.15, f32[16,4,128,128]{3,2,1,0:T(8,128)S(1)} %copy-done.4, f32[16,4]{1,0:T(8,128)S(1)} %copy.68), kind=kOutput, calls=%fused_computation.5 | convolution fusion | flops 1612447744 | bytes 9437440 | tf_op jit(solution)/shard_map/gnac,gndc->gnad/dot_general | solution.py:36
  383.4 2.9 broadcast_multiply_fusion
  386.3 2.7 copy.45
  389.0 2.5 copy.46
  391.5 2.3 fusion.4
  (61 shorter events, 15.2 us)
Async XLA Ops:
  7.2 3.3 copy-start
  18.6 151.2 %all-to-all-start = ((bf16[64,3,128,128]{3,2,1,0:T(8,128)(2,1)}), bf16[64,3,128,128]{3,2,1,0:T(8,128)(2,1)}, u32[]{:S(2)}, u32[]{:S(2)}) async-start(bf16[64,3,128,128]{3,2,1,0:T(8,128)(2,1)} %bitcast.54), calls=%async_computation | async-start | bytes 12582912 | tf_op jit(solution)/shard_map/all_to_all | solution.py:74
  30.9 198.4 %all-reduce.2.cloned.1.call-start = ((), (), s32[]{:S(2)}) async-start(), calls=%async_computation.1 | async-start | bytes 2097152 | tf_op jit(solution)/shard_map/psum | solution.py:96
  175.6 5.5 %copy-start.11 = (s32[16]{0:T(128)S(1)}, s32[16]{0:T(128)}, u32[]{:S(2)}) copy-start(s32[16]{0:T(128)} %param.16) | copy-start | bytes 196
  181.2 49.8 %copy-start.7 = (f32[16,128]{1,0:T(8,128)S(1)}, f32[16,128]{1,0:T(8,128)}, u32[]{:S(2)}) copy-start(f32[16,128]{1,0:T(8,128)} %param.14) | copy-start | bytes 24580
  181.2 49.8 %copy-start.8 = (f32[16]{0:T(128)S(1)}, f32[16]{0:T(128)}, u32[]{:S(2)}) copy-start(f32[16]{0:T(128)} %param.15) | copy-start | bytes 196
  181.9 56.7 %copy-start.10 = (s32[16,4]{0,1:T(4,128)S(1)}, s32[16,4]{0,1:T(4,128)}, u32[]{:S(2)}) copy-start(s32[16,4]{0,1:T(4,128)} %param.17) | copy-start | bytes 772
  181.9 56.9 %copy-start.9 = (f32[16,4]{0,1:T(4,128)S(1)}, f32[16,4]{0,1:T(4,128)}, u32[]{:S(2)}) copy-start(f32[16,4]{0,1:T(4,128)} %param.18) | copy-start | bytes 772
  230.6 27.7 %copy-start.5 = (f32[16,128,128]{2,1,0:T(8,128)}, f32[16,128,128]{2,1,0:T(8,128)S(1)}, u32[]{:S(2)}) copy-start(f32[16,128,128]{2,1,0:T(8,128)S(1)} %mul.59) | copy-start | bytes 3145732
  231.4 16.8 %collective-permute-start = (f32[16,128,128]{1,2,0:T(8,128)S(1)}, f32[16,128,128]{1,2,0:T(8,128)}, u32[]{:S(2)}, u32[]{:S(2)}) collective-permute-start(f32[16,128,128]{1,2,0:T(8,128)S(1)} %fusion.5), channel_id=1, source_target_pairs={{0,4},{4,8},{8,12},{12,16},{16,20},{20,24},{24,28},{28,32},{32,36}... | collective-permute-start | bytes 3145736 | tf_op jit(solution)/shard_map/ppermute | solution.py:20
  236.5 18.3 %collective-permute-start.1 = (f32[16,128,128]{1,2,0:T(8,128)S(1)}, f32[16,128,128]{1,2,0:T(8,128)}, u32[]{:S(2)}, u32[]{:S(2)}) collective-permute-start(f32[16,128,128]{1,2,0:T(8,128)S(1)} %fusion.5), channel_id=1, source_target_pairs={{4,0},{8,4},{12,8},{16,12},{20,16},{24,20},{28,24},{32,28},{36,32}... | collective-permute-start | bytes 3145736 | tf_op jit(solution)/shard_map/ppermute | solution.py:22
  263.0 12.0 %copy-start.2 = (f32[16,4,128,128]{3,2,1,0:T(8,128)S(1)}, f32[16,4,128,128]{3,2,1,0:T(8,128)}, u32[]{:S(2)}) copy-start(f32[16,4,128,128]{3,2,1,0:T(8,128)} %param.19) | copy-start | bytes 12582916
  285.2 13.7 %collective-permute-start.2 = (f32[16,128,128]{1,2,0:T(8,128)S(1)}, f32[16,128,128]{1,2,0:T(8,128)S(1)}, u32[]{:S(2)}, u32[]{:S(2)}) collective-permute-start(f32[16,128,128]{1,2,0:T(8,128)S(1)} %fusion), channel_id=1, source_target_pairs={{0,4},{4,8},{8,12},{12,16},{16,20},{20,24},{24,28},{28,32},{32,36}... | collective-permute-start | bytes 3145736 | tf_op jit(solution)/shard_map/ppermute | solution.py:20
  287.1 18.2 %collective-permute-start.3 = (f32[16,128,128]{1,2,0:T(8,128)S(1)}, f32[16,128,128]{1,2,0:T(8,128)S(1)}, u32[]{:S(2)}, u32[]{:S(2)}) collective-permute-start(f32[16,128,128]{1,2,0:T(8,128)S(1)} %fusion), channel_id=1, source_target_pairs={{4,0},{8,4},{12,8},{16,12},{20,16},{24,20},{28,24},{32,28},{36,32}... | collective-permute-start | bytes 3145736 | tf_op jit(solution)/shard_map/ppermute | solution.py:22
  312.0 12.0 %copy-start.3 = (f32[16,4,128,128]{3,2,1,0:T(8,128)S(1)}, f32[16,4,128,128]{3,2,1,0:T(8,128)}, u32[]{:S(2)}) copy-start(f32[16,4,128,128]{3,2,1,0:T(8,128)} %param.19) | copy-start | bytes 12582916
  334.2 13.7 %collective-permute-start.4 = (f32[16,128,128]{1,2,0:T(8,128)S(1)}, f32[16,128,128]{1,2,0:T(8,128)S(1)}, u32[]{:S(2)}, u32[]{:S(2)}) collective-permute-start(f32[16,128,128]{1,2,0:T(8,128)S(1)} %fusion.1), channel_id=1, source_target_pairs={{0,4},{4,8},{8,12},{12,16},{16,20},{20,24},{24,28},{28,32},{32,36}... | collective-permute-start | bytes 3145736 | tf_op jit(solution)/shard_map/ppermute | solution.py:20
  336.1 18.2 %collective-permute-start.5 = (f32[16,128,128]{1,2,0:T(8,128)S(1)}, f32[16,128,128]{1,2,0:T(8,128)S(1)}, u32[]{:S(2)}, u32[]{:S(2)}) collective-permute-start(f32[16,128,128]{1,2,0:T(8,128)S(1)} %fusion.1), channel_id=1, source_target_pairs={{4,0},{8,4},{12,8},{16,12},{20,16},{24,20},{28,24},{32,28},{36,32}... | collective-permute-start | bytes 3145736 | tf_op jit(solution)/shard_map/ppermute | solution.py:22
  361.0 12.0 %copy-start.4 = (f32[16,4,128,128]{3,2,1,0:T(8,128)S(1)}, f32[16,4,128,128]{3,2,1,0:T(8,128)}, u32[]{:S(2)}) copy-start(f32[16,4,128,128]{3,2,1,0:T(8,128)} %param.19) | copy-start | bytes 12582916
  383.4 10.4 %copy-start.1 = (bf16[64,128,128]{2,1,0:T(8,128)(2,1)S(1)}, bf16[64,128,128]{2,1,0:T(8,128)(2,1)}, u32[]{:S(2)}) copy-start(bf16[64,128,128]{2,1,0:T(8,128)(2,1)} %param.10) | copy-start | bytes 6291460
  386.3 5.2 %copy-start.6 = (f32[16,128,128]{2,1,0:T(8,128)S(1)}, f32[16,128,128]{2,1,0:T(8,128)}, u32[]{:S(2)}) copy-start(f32[16,128,128]{2,1,0:T(8,128)} %copy-done.5) | copy-start | bytes 3145732
Sparse Core Ops, SparseCore 0:
  181.2 48.0 all-reduce.1
where the time goes:
time: 405 us; the launch traced here: 401 us
  waiting for transfers between devices  233 us (58%)
  matrix products  68.6 us (17%)
  local copies, waits for them, and re-layouts  38.8 us (10%)
  starting transfers between devices  28.7 us (7%)
  other arithmetic  17.1 us (4%)
  between operations  14.4 us (4%)
    all_to_all x1, waiting for transfers between devices, shards(): lax.all_to_all(outgoing, 'pair', split_axis=0, concat_axis=0, tiled=True)  139 us
    psum x1, waiting for transfers between devices, shards(): integrals = mask * lax.psum(partial_ints, 'aux')  47.4 us
    dot_general x3, matrix products, couple_rows(): first = jnp.einsum('gnab,gnbc->gnac', intersections, near, precision=HIGH)  36 us
    ppermute x3, waiting for transfers between devices, with_halo(): lax.ppermute(tail, axis, [(i, (i + 1) % count) for i in range(ends)])  27.4 us
    dot_general x3, matrix products, couple_rows(): second = jnp.einsum('gnac,gndc->gnad', first, intersections, precision=HIGH)  27.2 us
    ppermute x3, waiting for transfers between devices, with_halo(): lax.ppermute(head, axis, [((i + 1) % count, i) for i in range(ends)])  19.6 us
    gather x3, local copies, waits for them, and re-layouts, couple_rows(): near = window[near_index]  13.9 us
    all_to_all x1, starting transfers between devices, shards(): lax.all_to_all(outgoing, 'pair', split_axis=0, concat_axis=0, tiled=True)  12.4 us
  transfers between devices with their start and end apart: 8, of which 8 were waited for; matrix products, arithmetic and copies ran while one was open for 0% of the time, Pallas kernels for 0%

commit v1 on v0

v1 whole, which is shorter than its diff:
```python
import functools

import jax
import jax.numpy as jnp
from jax import lax
from jax.experimental import pallas as pl
from jax.experimental.pallas import tpu as pltpu
from jax.sharding import PartitionSpec as P

ITERS = 3
MESH = pl.DeviceIdType.MESH

PLANES = 8
COLS = 8
OWNERS = PLANES * COLS
AUXES = 4
PAIRS = 16
REQ = 8
TOTAL = PAIRS * REQ
TILE = 128
CAP = 3
DIRECT = 2
EXTRA = 2

VMEM_LIMIT = 56 * 2**20


def distance(step):
    dz, dy, _ = step
    return min(dz, PLANES - dz) + min(dy, 4 - dy)


STEPS = sorted(
    [(dz, dy, dc) for dz in range(PLANES) for dy in range(4) for dc in range(2) if (dz, dy, dc) != (0, 0, 0)],
    key=lambda s: -distance(s),
)


def exchange_kernel(
    send_pos, relay_row, land_row, blocks, coef_hbm, out,
    coef, outgoing, landing, relay_out, relay_in, extra_out, coef_sem, sems,
):
    me, ax = lax.axis_index("pair"), lax.axis_index("aux")
    plane, col = me // COLS, me % COLS
    y, core = col // 2, col % 2

    barrier = pltpu.get_barrier_semaphore()

    def greet(k, carry):
        pl.semaphore_signal(barrier, inc=1, device_id=(lax.rem(me + k, OWNERS), ax), device_id_type=MESH)
        return carry

    lax.fori_loop(1, OWNERS, greet, 0)
    coef_copy = pltpu.make_async_copy(coef_hbm, coef, coef_sem)
    coef_copy.start()

    def fill(k, carry):
        dst = lax.rem(me + k, OWNERS)
        for s in range(DIRECT):
            outgoing[DIRECT * k + s] = blocks[send_pos[dst * CAP + s]]
        return carry

    lax.fori_loop(0, OWNERS, fill, 0)

    def fill_relay(i, carry):
        k, b = i // PLANES, i % PLANES
        dst = b * COLS + lax.rem(col + k, COLS)
        relay_out[i] = blocks[send_pos[dst * CAP + DIRECT]]
        return carry

    lax.fori_loop(0, OWNERS, fill_relay, 0)
    for s in range(DIRECT):
        landing[s] = outgoing[s]
    for b in range(PLANES):
        relay_in[b] = relay_out[b]
    pl.semaphore_wait(barrier, OWNERS - 1)

    def direct(dst):
        to, back = lax.rem(dst - me + OWNERS, OWNERS), lax.rem(me - dst + OWNERS, OWNERS)
        return pltpu.make_async_remote_copy(
            src_ref=outgoing.at[pl.ds(DIRECT * to, DIRECT)],
            dst_ref=landing.at[pl.ds(DIRECT * back, DIRECT)],
            send_sem=sems.at[0], recv_sem=sems.at[1],
            device_id=(dst, ax), device_id_type=MESH,
        )

    def to_relay(k):
        return pltpu.make_async_remote_copy(
            src_ref=relay_out.at[pl.ds(PLANES * k, PLANES)],
            dst_ref=relay_in.at[pl.ds(PLANES * (COLS - k), PLANES)],
            send_sem=sems.at[2], recv_sem=sems.at[3],
            device_id=(plane * COLS + lax.rem(col + k, COLS), ax), device_id_type=MESH,
        )

    def from_relay(k):
        return pltpu.make_async_remote_copy(
            src_ref=extra_out.at[pl.ds(EXTRA * k, EXTRA)],
            dst_ref=landing.at[pl.ds(DIRECT * OWNERS + EXTRA * (PLANES - k), EXTRA)],
            send_sem=sems.at[4], recv_sem=sems.at[5],
            device_id=(lax.rem(plane + k, PLANES) * COLS + col, ax), device_id_type=MESH,
        )

    for k in range(1, COLS):
        to_relay(k).start()
    for dz, dy, dc in STEPS:
        direct(
            lax.rem(plane + dz, PLANES) * COLS + lax.rem(y + dy, 4) * 2 + lax.rem(core + dc, 2)
        ).start()

    def whole(source, target, first, count, sem):
        return pltpu.make_async_remote_copy(
            src_ref=source.at[pl.ds(first, count)], dst_ref=target.at[pl.ds(first, count)],
            send_sem=sems.at[sem], recv_sem=sems.at[sem + 1],
            device_id=(lax.rem(me + 1, OWNERS), ax), device_id_type=MESH,
        )

    relayed = whole(relay_out, relay_in, PLANES, PLANES * (COLS - 1), 2)
    relayed.wait_recv()
    for k in (4, 3, 5, 2, 6, 1, 7, 0):
        b = lax.rem(plane + k, PLANES)
        for e in range(EXTRA):
            block = relay_in[relay_row[b * EXTRA + e]]
            if k == 0:
                landing[DIRECT * OWNERS + e] = block
            else:
                extra_out[EXTRA * k + e] = block
        if k != 0:
            from_relay(k).start()

    coef_copy.wait()
    relayed.wait_send()
    sent = whole(outgoing, landing, DIRECT, DIRECT * (OWNERS - 1), 0)
    sent.wait_send()
    sent.wait_recv()
    extras = pltpu.make_async_remote_copy(
        src_ref=extra_out.at[pl.ds(EXTRA, EXTRA * (PLANES - 1))],
        dst_ref=landing.at[pl.ds(DIRECT * OWNERS + EXTRA, EXTRA * (PLANES - 1))],
        send_sem=sems.at[4], recv_sem=sems.at[5],
        device_id=(lax.rem(me + 1, OWNERS), ax), device_id_type=MESH,
    )
    extras.wait_send()
    extras.wait_recv()

    def build(q, carry):
        halves = []
        for m in range(2):
            total = None
            for t in range(REQ // 2):
                term = jnp.dot(
                    landing[land_row[q * REQ + m * (REQ // 2) + t]],
                    coef[q, t * TILE : (t + 1) * TILE, :],
                    preferred_element_type=jnp.float32,
                )
                total = term if total is None else total + term
            halves.append(total.astype(jnp.bfloat16))
        out[q] = lax.dot_general(
            halves[0], halves[1], (((0,), (0,)), ((), ())), preferred_element_type=jnp.float32
        )
        return carry

    lax.fori_loop(0, PAIRS, build, 0)


def exchange(blocks, coef, send_pos, relay_row, land_row):
    smem, vmem = pl.BlockSpec(memory_space=pltpu.SMEM), pl.BlockSpec(memory_space=pltpu.VMEM)
    tiles = lambda n: pltpu.VMEM((n, TILE, TILE), jnp.bfloat16)
    return pl.pallas_call(
        exchange_kernel,
        out_shape=jax.ShapeDtypeStruct((PAIRS, TILE, TILE), jnp.float32),
        in_specs=[smem, smem, smem, vmem, pl.BlockSpec(memory_space=pl.ANY)],
        out_specs=vmem,
        scratch_shapes=[
            pltpu.VMEM(coef.shape, jnp.bfloat16),
            tiles(DIRECT * OWNERS),
            tiles(DIRECT * OWNERS + EXTRA * PLANES),
            tiles(OWNERS),
            tiles(OWNERS),
            tiles(EXTRA * PLANES),
            pltpu.SemaphoreType.DMA,
            pltpu.SemaphoreType.DMA((6,)),
        ],
        compiler_params=pltpu.CompilerParams(
            collective_id=0, has_side_effects=True, vmem_limit_bytes=VMEM_LIMIT
        ),
    )(send_pos, relay_row, land_row, blocks, coef)


def padded_exchange(blocks, coef, send_pos, own_source, own_rank):
    incoming = lax.all_to_all(
        blocks[send_pos], "pair", split_axis=0, concat_axis=0, tiled=True
    )
    arrived = incoming.reshape((OWNERS * CAP,) + blocks.shape[1:])[own_source * CAP + own_rank]
    arrived = arrived.reshape((PAIRS, 2, REQ // 2) + blocks.shape[1:])
    coefs = coef.reshape(PAIRS, REQ // 2, TILE, TILE)
    projected = jnp.einsum(
        "qmtxp,qtpn->qmxn", arrived, coefs, preferred_element_type=jnp.float32
    ).astype(jnp.bfloat16)
    return jnp.einsum(
        "qxa,qxb->qab", projected[:, 0], projected[:, 1], preferred_element_type=jnp.float32
    )


def route(source_dev, block_pos, me):
    plane, col = me // COLS, me % COLS
    source = source_dev.reshape(OWNERS, TOTAL)
    position = block_pos.reshape(OWNERS, TOTAL)
    slots = jnp.arange(CAP, dtype=jnp.int32)
    devices = jnp.arange(OWNERS, dtype=jnp.int32)
    wanted = source == me
    ranking = jnp.cumsum(wanted.astype(jnp.int32), axis=1) - 1
    chosen = wanted[:, None, :] & (ranking[:, None, :] == slots[None, :, None])
    send_pos = jnp.sum(jnp.where(chosen, position[:, None, :], 0), axis=2)
    taken = jnp.sum((source[:, None, :] == devices[None, :, None]).astype(jnp.int32), axis=2)
    third = (taken > DIRECT).astype(jnp.int32)
    fits = jnp.max(jnp.sum(third.reshape(OWNERS, PLANES, COLS), axis=2)) <= EXTRA
    own_source = lax.dynamic_index_in_dim(source, me, 0, keepdims=False)
    order = jnp.arange(TOTAL, dtype=jnp.int32)
    earlier = (own_source[None, :] == own_source[:, None]) & (order[None, :] < order[:, None])
    own_rank = jnp.sum(earlier.astype(jnp.int32), axis=1)
    own_third = lax.dynamic_index_in_dim(third, me, 0, keepdims=False)
    before = (devices[None, :] < own_source[:, None]) & (
        devices[None, :] // COLS == own_source[:, None] // COLS
    )
    extra_rank = jnp.sum(jnp.where(before, own_third[None, :], 0), axis=1)
    extra_row = (
        DIRECT * OWNERS
        + lax.rem(own_source // COLS - plane + PLANES, PLANES) * EXTRA
        + jnp.minimum(extra_rank, EXTRA - 1)
    )
    direct_row = lax.rem(own_source - me + OWNERS, OWNERS) * DIRECT + own_rank
    land_row = jnp.where(own_rank >= DIRECT, extra_row, direct_row)
    column = lax.dynamic_index_in_dim(third.reshape(PLANES, COLS, PLANES, COLS), col, 1, keepdims=False)
    column = lax.dynamic_index_in_dim(column, plane, 1, keepdims=False)
    cols = jnp.arange(COLS, dtype=jnp.int32)
    place = jnp.cumsum(column, axis=1) - column
    hit = (column == 1)[:, None, :] & (place[:, None, :] == jnp.arange(EXTRA)[None, :, None])
    back = lax.rem(cols - col + COLS, COLS)
    relay_row = jnp.sum(jnp.where(hit, back[None, None, :], 0), axis=2) * PLANES + cols[:, None]
    return send_pos, relay_row, land_row, own_source, own_rank, fits


def sweep_kernel(
    near, weight, count, occ, partial, energy, inter_hbm, amp, pair_energy,
    inter, vecs, window0, window1, window2, integ, inverse, sums, inter_sem, rs_send, rs_recv, ag_send, ag_recv, halo_send, halo_recv,
):
    me, ax = lax.axis_index("pair"), lax.axis_index("aux")
    left, right = lax.rem(me + OWNERS - 1, OWNERS), lax.rem(me + 1, OWNERS)
    chunk = PAIRS // AUXES
    own = pl.multiple_of(ax * chunk, chunk)
    peers = [lax.rem(ax + r, AUXES) for r in range(AUXES)]
    windows = (window0, window1, window2)

    barrier = pltpu.get_barrier_semaphore()
    for r in range(1, AUXES):
        pl.semaphore_signal(barrier, inc=1, device_id=(me, peers[r]), device_id_type=MESH)
    for side in (left, right):
        pl.semaphore_signal(barrier, inc=1, device_id=(side, ax), device_id_type=MESH)
    inter_copy = pltpu.make_async_copy(inter_hbm, inter, inter_sem)
    inter_copy.start()
    pl.semaphore_wait(barrier, AUXES + 1)

    def reduce_copy(r):
        return pltpu.make_async_remote_copy(
            src_ref=partial.at[pl.ds(peers[r] * chunk, chunk)], dst_ref=sums.at[AUXES - 1 - r],
            send_sem=rs_send.at[r - 1], recv_sem=rs_recv.at[AUXES - 1 - r],
            device_id=(me, peers[r]), device_id_type=MESH,
        )

    def gather_copy(r):
        return pltpu.make_async_remote_copy(
            src_ref=integ.at[pl.ds(own, chunk)], dst_ref=integ.at[pl.ds(own, chunk)],
            send_sem=ag_send.at[r - 1], recv_sem=ag_recv.at[AUXES - 1 - r],
            device_id=(me, peers[r]), device_id_type=MESH,
        )

    def halo_copy(sweep, first, size, side):
        target = first + 2 * PAIRS if side == 0 else first
        return pltpu.make_async_remote_copy(
            src_ref=windows[sweep].at[pl.ds(PAIRS + first, size)],
            dst_ref=windows[sweep].at[pl.ds(target, size)],
            send_sem=halo_send.at[sweep, side], recv_sem=halo_recv.at[sweep, side],
            device_id=(left if side == 0 else right, ax), device_id_type=MESH,
        )

    def halo_wait(sweep):
        for side in range(2):
            done = pltpu.make_async_remote_copy(
                src_ref=windows[sweep].at[pl.ds(PAIRS, PAIRS)],
                dst_ref=windows[sweep].at[pl.ds(2 * PAIRS if side == 0 else 0, PAIRS)],
                send_sem=halo_send.at[sweep, side], recv_sem=halo_recv.at[sweep, side],
                device_id=(left if side == 0 else right, ax), device_id_type=MESH,
            )
            done.wait_send()
            done.wait_recv()

    for r in (2, 1, 3):
        reduce_copy(r).start()

    rows = lax.broadcasted_iota(jnp.int32, (TILE, TILE), 0)
    columns = lax.broadcasted_iota(jnp.int32, (TILE, TILE), 1)

    def denominators(q, carry):
        e = energy[pl.ds(q, 1), :]
        across = jnp.broadcast_to(e, (TILE, TILE))
        denom = across + across.T + occ[q]
        live = (rows < count[q]) & (columns < count[q])
        inverse[q] = jnp.where(live, 1.0 / denom, 0.0)
        return carry

    lax.fori_loop(0, PAIRS, denominators, 0)
    inter_copy.wait()

    def narrow(q, carry):
        vecs[q] = inter[q].astype(jnp.bfloat16)
        return carry

    lax.fori_loop(0, PAIRS, narrow, 0)

    for r in (1, 3, 2):
        reduce_copy(r).wait_recv()

    def add(i, carry):
        q = own + i
        live = (rows < count[q]) & (columns < count[q])
        integ[q] = jnp.where(live, partial[q] + sums[0, i] + sums[1, i] + sums[2, i], 0.0)
        return carry

    lax.fori_loop(0, chunk, add, 0)
    for r in (2, 1, 3):
        gather_copy(r).start()

    def first_amplitudes(start):
        def body(i, carry):
            q = start + i
            window0[PAIRS + q] = (-integ[q] * inverse[q]).astype(jnp.bfloat16)
            return carry

        lax.fori_loop(0, chunk, body, 0)
        for side in range(2):
            halo_copy(0, start, chunk, side).start()

    first_amplitudes(own)
    for r in (1, 3, 2):
        arrived = pltpu.make_async_remote_copy(
            src_ref=integ.at[pl.ds(own, chunk)], dst_ref=integ.at[pl.ds(peers[r] * chunk, chunk)],
            send_sem=ag_send.at[r - 1], recv_sem=ag_recv.at[r - 1],
            device_id=(me, peers[r]), device_id_type=MESH,
        )
        arrived.wait_recv()
        first_amplitudes(pl.multiple_of(peers[r] * chunk, chunk))

    for sweep in range(ITERS):
        halo_wait(sweep)

        def update(q, sweep=sweep):
            total = None
            for n in range(4):
                v = vecs[q, n]
                first = jnp.dot(v, windows[sweep][near[q * 4 + n]], preferred_element_type=jnp.float32)
                first = (first * weight[q * 4 + n]).astype(jnp.bfloat16)
                second = lax.dot_general(
                    first, v, (((1,), (1,)), ((), ())), preferred_element_type=jnp.float32
                )
                total = second if total is None else total + second
            integrals = integ[q]
            current = (total - integrals) * inverse[q]
            if sweep < ITERS - 1:
                windows[sweep + 1][PAIRS + q] = current.astype(jnp.bfloat16)
            else:
                amp[q] = current
                pair_energy[q] = jnp.sum(integrals * (2.0 * current - current.T))

        for j in range(AUXES):
            def body(i, carry, j=j):
                update(j * chunk + i)
                return carry

            lax.fori_loop(0, chunk, body, 0)
            if sweep < ITERS - 1:
                for side in range(2):
                    halo_copy(sweep + 1, j * chunk, chunk, side).start()

    for r in range(1, AUXES):
        reduce_copy(r).wait_send()
        gather_copy(r).wait_send()


def sweeps(partial, energy, occ, count, near, weight, inter):
    smem, vmem = pl.BlockSpec(memory_space=pltpu.SMEM), pl.BlockSpec(memory_space=pltpu.VMEM)
    f32, bf16 = jnp.float32, jnp.bfloat16
    chunk = PAIRS // AUXES
    dma = pltpu.SemaphoreType.DMA
    return pl.pallas_call(
        sweep_kernel,
        out_shape=(
            jax.ShapeDtypeStruct((PAIRS, TILE, TILE), f32),
            jax.ShapeDtypeStruct((PAIRS,), f32),
        ),
        in_specs=[smem, smem, smem, smem, vmem, vmem, pl.BlockSpec(memory_space=pl.ANY)],
        out_specs=(vmem, smem),
        scratch_shapes=[
            pltpu.VMEM(inter.shape, f32),
            pltpu.VMEM(inter.shape, bf16),
            *[pltpu.VMEM((3 * PAIRS, TILE, TILE), bf16)] * ITERS,
            pltpu.VMEM((PAIRS, TILE, TILE), f32),
            pltpu.VMEM((PAIRS, TILE, TILE), f32),
            pltpu.VMEM((AUXES - 1, chunk, TILE, TILE), f32),
            dma,
            dma((AUXES - 1,)), dma((AUXES - 1,)), dma((AUXES - 1,)), dma((AUXES - 1,)),
            dma((ITERS, 2)), dma((ITERS, 2)),
        ],
        compiler_params=pltpu.CompilerParams(
            collective_id=1, has_side_effects=True, vmem_limit_bytes=VMEM_LIMIT
        ),
    )(near, weight, count, occ, partial, energy, inter)


def shards(
    blocks, pno_coef, source_dev, block_pos, pno_energy, occ_energy, pno_count, neighbour, coupling, intersection,
):
    me = lax.axis_index("pair")
    send_pos, relay_row, land_row, own_source, own_rank, fits = route(source_dev, block_pos, me)
    partial = lax.cond(
        fits,
        lambda: exchange(blocks, pno_coef, send_pos.reshape(-1), relay_row.reshape(-1), land_row),
        lambda: padded_exchange(blocks, pno_coef, send_pos, own_source, own_rank),
    )
    near = neighbour - (me - 1) * PAIRS
    return sweeps(
        partial, pno_energy, occ_energy, pno_count, near.reshape(-1), coupling.reshape(-1), intersection
    )


def solution(mesh):
    return jax.shard_map(
        shards,
        mesh=mesh,
        in_specs=(
            P("pair", "aux", None),
            P("pair", None, None),
            P(),
            P(),
            P("pair", None),
            P("pair"),
            P("pair"),
            P("pair", None),
            P("pair", None),
            P("pair", None, None, None),
        ),
        out_specs=(P("pair", None, None), P("pair")),
        check_vma=False,
    )
```

time: 405 us -> 211 us (0.52)
  waiting for transfers between devices: 233 us -> 0 us
  Pallas kernels: 0 us -> 193 us
  matrix products: 68.6 us -> 0 us
  local copies, waits for them, and re-layouts: 38.8 us -> 9 us
  starting transfers between devices: 28.7 us -> 0 us
  other arithmetic: 17.1 us -> 3.58 us
  between operations: 14.4 us -> 1.5 us
    pallas_call x0 -> x2, Pallas kernels: none -> 193 us  [the longest x1 119 us: exchange(): pl.pallas_call(exchange_kernel, out_shape=jax.ShapeDtypeStruct((PAIRS, TI...]
    all_to_all x1 -> x0, waiting for transfers between devices: 139 us -> none  [shards(): lax.all_to_all(outgoing, 'pair', split_axis=0, concat_axis=0, tiled=True)]
    dot_general x8 -> x0, matrix products: 68.6 us -> none  [the longest x3 36 us: couple_rows(): first = jnp.einsum('gnab,gnbc->gnac', intersections, near, precision=HIGH)]
    psum x1 -> x0, waiting for transfers between devices: 47.4 us -> none  [shards(): integrals = mask * lax.psum(partial_ints, 'aux')]
    ppermute x6 -> x0, waiting for transfers between devices: 47.1 us -> none  [the longest x3 27.4 us: with_halo(): lax.ppermute(tail, axis, [(i, (i + 1) % count) for i in range(ends)])]
    gather x5 -> x0, local copies, waits for them, and re-layouts: 27.9 us -> none  [the longest x3 13.9 us: couple_rows(): near = window[near_index]]
    ppermute x6 -> x0, starting transfers between devices: 16.3 us -> none  [the longest x3 8.89 us: with_halo(): lax.ppermute(tail, axis, [(i, (i + 1) % count) for i in range(ends)])]
    all_to_all x1 -> x0, starting transfers between devices: 12.4 us -> none  [shards(): lax.all_to_all(outgoing, 'pair', split_axis=0, concat_axis=0, tiled=True)]
  transfers between devices with their start and end apart: 8 -> 0, of which waited for: 8 -> 0; matrix products, arithmetic and copies ran while one was open for 0% -> 0% of each run, Pallas kernels for 0% -> 0%
where the time goes in v1:
time: 211 us; the launch traced here: 207 us
  Pallas kernels  193 us (91%)
  local copies, waits for them, and re-layouts  9 us (4%)
  other arithmetic  3.58 us (2%)
    pallas_call x1, Pallas kernels, exchange(): pl.pallas_call(exchange_kernel, out_shape=jax.ShapeDtypeStruct((PAIRS, TI...  119 us
    pallas_call x1, Pallas kernels, sweeps(): pl.pallas_call(sweep_kernel, out_shape=(jax.ShapeDtypeStruct((PAIRS, TILE...  73.8 us
    unnamed x9, local copies, waits for them, and re-layouts  5.48 us

profile of v1, /device:TPU:25, one launch (start us, length us, event | category | flops | bytes accessed | tf_op | source)
XLA Modules:
  0.0 207.4 jit_solution(9697967867610616429)
XLA Ops:
  0.7 1.0 copy.32
  1.6 0.3 eq.105
  1.9 1.2 convert_reduce_fusion
  3.1 0.1 reshape.184
  3.2 0.2 reduce_window_sum.23
  3.4 0.2 convert_reduce_fusion.1
  3.6 0.3 reduce_window_sum.22
  3.9 1.0 copy.34
  4.9 0.3 broadcast_in_dim.74
  5.1 0.2 select_reduce_fusion.1
  5.3 0.1 copy.33
  5.4 0.6 reduce_max.9
  6.7 0.0 copy-start.2
  6.7 0.0 copy-start.1
  6.7 122.0 %conditional.1 = (f32[16,128,128]{2,1,0:T(8,128)S(1)}) conditional(s32[]{:T(128)} %convert_element_type.37, (s32[64,3]{0,1:T(4,128)S(1)}, bf16[64,128,128]{2,1,0:T(8,128)(2,1)}, s32[128]{0:T(128)S(1)}, s32[128]{0:T(128)S(1)}, bf16[16,512,128]{2,1,0:T(8,128)(2,1)}) %tuple.69, (s32[64,3]{0,1:T(4,128)S(1)}, s32[8,1,8]{2,0,1:T(8,128)S(1)}, ...), branch_computations={%region_7.8_spmd, %region_8.11_spmd} | conditional | flops 604507328 | bytes 57688644 | solution.py:423
  6.8 0.2 select_reduce_fusion
  7.0 0.5 compare_select_fusion.2.land_row
  7.5 0.2 fusion
  7.8 0.7 reshape.178.relay_row
  8.4 0.1 copy.36
  8.5 0.7 reshape.177.send_pos
  9.2 119.3 %branch_1_fun.1 = f32[16,128,128]{2,1,0:T(8,128)S(1)} custom-call(s32[192]{0:T(256)} %reshape.177.send_pos, s32[16]{0:T(128)} %reshape.178.relay_row, s32[128]{0:T(128)} %compare_select_fusion.2.land_row, bf16[64,128,128]{2,1,0:T(8,128)(2,1)} %get-tuple-element.267.blocks, bf16[16,512,128]{2,1,0:T(8,128)(2,1)} %get-tuple-element.268.coef_hbm), custom_call_target="tpu_custom_call" | custom-call | tf_op jit(solution)/shard_map/cond/branch_1_fun/pallas_call | solution.py:167
  128.8 0.0 copy-done.2
  128.8 0.1 copy.30
  128.9 0.6 reshape.181.near
  129.5 0.0 copy-done.1
  129.5 0.1 copy.31
  129.6 0.6 reshape.182.weight
  130.2 73.8 %shard_map.113 = (f32[16,128,128]{2,1,0:T(8,128)}, f32[16]{0:T(128)}) custom-call(s32[64]{0:T(128)} %reshape.181.near, f32[64]{0:T(128)} %reshape.182.weight, s32[16]{0:T(128)} %count.1, f32[16]{0:T(128)} %occ.1, f32[16,128,128]{2,1,0:T(8,128)S(1)} %get-tuple-element.390.partial, f32[16,128]{1,0:T(8,128)} %energy.1, f32[16,4,128,128]{3,2,1,0:T(8,128)} %inter_hbm.1), custom_call_target="tpu_custom_call" | custom-call | tf_op jit(solution)/shard_map/pallas_call | solution.py:393
  203.9 2.3 %copy.44 = f32[16,128,128]{2,1,0:T(8,128)} copy(f32[16,128,128]{2,1,0:T(8,128)} %get-tuple-element.388) | data formatting | bytes 2097152
  206.2 1.2 copy.45
  (21 shorter events, 0.2 us)
Async XLA Ops:
  6.7 122.0 %copy-start.2 = (s32[16,4]{0,1:T(4,128)S(1)}, s32[16,4]{0,1:T(4,128)}, u32[]{:S(2)}) copy-start(s32[16,4]{0,1:T(4,128)} %param.19) | copy-start | bytes 772
  6.7 122.7 %copy-start.1 = (f32[16,4]{0,1:T(4,128)S(1)}, f32[16,4]{0,1:T(4,128)}, u32[]{:S(2)}) copy-start(f32[16,4]{0,1:T(4,128)} %param.20) | copy-start | bytes 772

commit v2 on v0

v2 whole, which is shorter than its diff:
```python
import functools
import types

import jax
import jax.numpy as jnp
from jax import lax
from jax.experimental import pallas as pl
from jax.experimental.pallas import tpu as pltpu
from jax.sharding import PartitionSpec as P

ITERS = 3
MESH = pl.DeviceIdType.MESH

PLANES = 8
COLS = 8
OWNERS = PLANES * COLS
AUXES = 4
PAIRS = 16
REQ = 8
DOM = 4
BLOCKS = 64
TOTAL = PAIRS * REQ
TILE = 128
CAP = 3
DIRECT = 2
EXTRA = 2

VMEM_LIMIT = 56 * 2**20
CHUNK = PAIRS // AUXES


def distance(step):
    dz, dy, _ = step
    return min(dz, PLANES - dz) + min(dy, 4 - dy)


STEPS = sorted(
    [(dz, dy, dc) for dz in range(PLANES) for dy in range(4) for dc in range(2) if (dz, dy, dc) != (0, 0, 0)],
    key=lambda s: -distance(s),
)


SCRATCH = {
    "inter": ((PAIRS, 4, TILE, TILE), jnp.float32),
    "vecs": ((PAIRS, TILE, 4 * TILE), jnp.bfloat16),
    "weighted": ((PAIRS, TILE, 4 * TILE), jnp.bfloat16),
    "window0": ((3 * PAIRS, TILE, TILE), jnp.bfloat16),
    "window1": ((3 * PAIRS, TILE, TILE), jnp.bfloat16),
    "window2": ((3 * PAIRS, TILE, TILE), jnp.bfloat16),
    "integ": ((PAIRS, TILE, TILE), jnp.float32),
    "inverse": ((PAIRS, TILE, TILE), jnp.float32),
    "own_part": ((CHUNK, TILE, TILE), jnp.float32),
    "high_out": ((AUXES - 1, CHUNK, TILE, TILE), jnp.bfloat16),
    "low_out": ((AUXES - 1, CHUNK, TILE, TILE), jnp.bfloat16),
    "high_in": ((AUXES - 1, CHUNK, TILE, TILE), jnp.bfloat16),
    "low_in": ((AUXES - 1, CHUNK, TILE, TILE), jnp.bfloat16),
    "high": ((PAIRS, TILE, TILE), jnp.bfloat16),
    "low": ((PAIRS, TILE, TILE), jnp.bfloat16),
    "local_sem": (2,),
    "x_send": (4, AUXES - 1),
    "x_recv": (4, AUXES - 1),
    "halo_send": (ITERS, 2),
    "halo_recv": (ITERS, 2),
}
EXCHANGE_SCRATCH = {
    "coef": ((PAIRS, DOM * TILE, TILE), jnp.bfloat16),
    "outgoing": ((DIRECT * OWNERS, TILE, TILE), jnp.bfloat16),
    "landing": ((DIRECT * OWNERS + EXTRA * PLANES, TILE, TILE), jnp.bfloat16),
    "relay_out": ((OWNERS, TILE, TILE), jnp.bfloat16),
    "relay_in": ((OWNERS, TILE, TILE), jnp.bfloat16),
    "extra_out": ((EXTRA * PLANES, TILE, TILE), jnp.bfloat16),
    "block_sem": (6,),
}
SEND, RELAY, LAND = 0, OWNERS * CAP, OWNERS * CAP + PLANES * EXTRA
NEAR = LAND + TOTAL
HIGH_SUM, HIGH_ALL, LOW_SUM, LOW_ALL = range(4)


def kernel(exchanging, *refs):
    names = ["table", "count", "occ", "source", "coef_hbm", "energy", "coupling", "inter_hbm", "amp", "pair_energy"]
    names += list(SCRATCH) + (list(EXCHANGE_SCRATCH) if exchanging else [])
    if not exchanging:
        names.remove("coef_hbm")
    r = types.SimpleNamespace(**dict(zip(names, refs, strict=True)))
    me, ax = lax.axis_index("pair"), lax.axis_index("aux")
    plane, col = me // COLS, me % COLS
    y, core = col // 2, col % 2
    left, right = lax.rem(me + OWNERS - 1, OWNERS), lax.rem(me + 1, OWNERS)
    own = pl.multiple_of(ax * CHUNK, CHUNK)
    peers = [lax.rem(ax + k, AUXES) for k in range(AUXES)]
    windows = (r.window0, r.window1, r.window2)

    barrier = pltpu.get_barrier_semaphore()
    for k in range(1, AUXES):
        pl.semaphore_signal(barrier, inc=1, device_id=(me, peers[k]), device_id_type=MESH)
    if exchanging:

        def greet(k, carry):
            pl.semaphore_signal(barrier, inc=1, device_id=(lax.rem(me + k, OWNERS), ax), device_id_type=MESH)
            return carry

        lax.fori_loop(1, OWNERS, greet, 0)
        greeted = AUXES - 1 + OWNERS - 1
    else:
        for side in (left, right):
            pl.semaphore_signal(barrier, inc=1, device_id=(side, ax), device_id_type=MESH)
        greeted = AUXES - 1 + 2

    inter_copy = pltpu.make_async_copy(r.inter_hbm, r.inter, r.local_sem.at[0])
    if exchanging:
        coef_copy = pltpu.make_async_copy(r.coef_hbm, r.coef, r.local_sem.at[1])

    rows = lax.broadcasted_iota(jnp.int32, (TILE, TILE), 0)
    columns = lax.broadcasted_iota(jnp.int32, (TILE, TILE), 1)

    def masked(q, values):
        return jnp.where((rows < r.count[q]) & (columns < r.count[q]), values, 0.0)

    def prepare():
        def denominators(q, carry):
            across = jnp.broadcast_to(r.energy[pl.ds(q, 1), :], (TILE, TILE))
            r.inverse[q] = masked(q, 1.0 / (across + across.T + r.occ[q]))
            return carry

        lax.fori_loop(0, PAIRS, denominators, 0)
        inter_copy.wait()

        def narrow(q, carry):
            for n in range(4):
                v = r.inter[q, n]
                cut = slice(n * TILE, (n + 1) * TILE)
                r.vecs[q, :, cut] = v.astype(jnp.bfloat16)
                r.weighted[q, :, cut] = (v * r.coupling[pl.ds(q, 1), n : n + 1]).astype(jnp.bfloat16)
            return carry

        lax.fori_loop(0, PAIRS, narrow, 0)

    if exchanging:
        blocks, outgoing, landing = r.source, r.outgoing, r.landing

        def fill(k, carry):
            dst = lax.rem(me + k, OWNERS)
            for s in range(DIRECT):
                outgoing[DIRECT * k + s] = blocks[r.table[SEND + dst * CAP + s]]
            return carry

        def fill_relay(i, carry):
            k, b = i // PLANES, i % PLANES
            dst = b * COLS + lax.rem(col + k, COLS)
            r.relay_out[i] = blocks[r.table[SEND + dst * CAP + DIRECT]]
            return carry

        lax.fori_loop(0, OWNERS, fill, 0)
        lax.fori_loop(0, OWNERS, fill_relay, 0)
        for s in range(DIRECT):
            landing[s] = outgoing[s]
        for b in range(PLANES):
            r.relay_in[b] = r.relay_out[b]

        def whole(source, target, first, count, sem):
            return pltpu.make_async_remote_copy(
                src_ref=source.at[pl.ds(first, count)], dst_ref=target.at[pl.ds(first, count)],
                send_sem=r.block_sem.at[sem], recv_sem=r.block_sem.at[sem + 1],
                device_id=(right, ax), device_id_type=MESH,
            )

        def direct(dst):
            to, back = lax.rem(dst - me + OWNERS, OWNERS), lax.rem(me - dst + OWNERS, OWNERS)
            return pltpu.make_async_remote_copy(
                src_ref=outgoing.at[pl.ds(DIRECT * to, DIRECT)],
                dst_ref=landing.at[pl.ds(DIRECT * back, DIRECT)],
                send_sem=r.block_sem.at[0], recv_sem=r.block_sem.at[1],
                device_id=(dst, ax), device_id_type=MESH,
            )

        def to_relay(k):
            return pltpu.make_async_remote_copy(
                src_ref=r.relay_out.at[pl.ds(PLANES * k, PLANES)],
                dst_ref=r.relay_in.at[pl.ds(PLANES * (COLS - k), PLANES)],
                send_sem=r.block_sem.at[2], recv_sem=r.block_sem.at[3],
                device_id=(plane * COLS + lax.rem(col + k, COLS), ax), device_id_type=MESH,
            )

        def from_relay(k):
            return pltpu.make_async_remote_copy(
                src_ref=r.extra_out.at[pl.ds(EXTRA * k, EXTRA)],
                dst_ref=landing.at[pl.ds(DIRECT * OWNERS + EXTRA * (PLANES - k), EXTRA)],
                send_sem=r.block_sem.at[4], recv_sem=r.block_sem.at[5],
                device_id=(lax.rem(plane + k, PLANES) * COLS + col, ax), device_id_type=MESH,
            )

        pl.semaphore_wait(barrier, greeted)
        for k in range(1, COLS):
            to_relay(k).start()
        for dz, dy, dc in STEPS:
            direct(
                lax.rem(plane + dz, PLANES) * COLS + lax.rem(y + dy, 4) * 2 + lax.rem(core + dc, 2)
            ).start()
        inter_copy.start()
        coef_copy.start()
        prepare()

        relayed = whole(r.relay_out, r.relay_in, PLANES, PLANES * (COLS - 1), 2)
        relayed.wait_recv()
        for k in (4, 3, 5, 2, 6, 1, 7, 0):
            b = lax.rem(plane + k, PLANES)
            for e in range(EXTRA):
                block = r.relay_in[r.table[RELAY + b * EXTRA + e]]
                if k == 0:
                    landing[DIRECT * OWNERS + e] = block
                else:
                    r.extra_out[EXTRA * k + e] = block
            if k != 0:
                from_relay(k).start()

        coef_copy.wait()
        relayed.wait_send()
        sent = whole(outgoing, landing, DIRECT, DIRECT * (OWNERS - 1), 0)
        sent.wait_send()
        sent.wait_recv()
        extras = pltpu.make_async_remote_copy(
            src_ref=r.extra_out.at[pl.ds(EXTRA, EXTRA * (PLANES - 1))],
            dst_ref=landing.at[pl.ds(DIRECT * OWNERS + EXTRA, EXTRA * (PLANES - 1))],
            send_sem=r.block_sem.at[4], recv_sem=r.block_sem.at[5],
            device_id=(right, ax), device_id_type=MESH,
        )
        extras.wait_send()
        extras.wait_recv()

        def part(q):
            rows_of = [
                jnp.concatenate(
                    [landing[r.table[LAND + q * REQ + m * DOM + t]] for t in range(DOM)], axis=1
                )
                for m in range(2)
            ]
            projected = jnp.dot(
                jnp.concatenate(rows_of, axis=0), r.coef[q], preferred_element_type=jnp.float32
            ).astype(jnp.bfloat16)
            return lax.dot_general(
                projected[:TILE], projected[TILE:], (((0,), (0,)), ((), ())),
                preferred_element_type=jnp.float32,
            )

    else:
        inter_copy.start()
        prepare()
        pl.semaphore_wait(barrier, greeted)

        def part(q):
            return r.source[q]

    def summed(kind, k):
        out, into = (r.high_out, r.high_in) if kind == HIGH_SUM else (r.low_out, r.low_in)
        return pltpu.make_async_remote_copy(
            src_ref=out.at[k - 1], dst_ref=into.at[AUXES - 1 - k],
            send_sem=r.x_send.at[kind, k - 1], recv_sem=r.x_recv.at[kind, AUXES - 1 - k],
            device_id=(me, peers[k]), device_id_type=MESH,
        )

    def spread(kind, k):
        values = r.high if kind == HIGH_ALL else r.low
        return pltpu.make_async_remote_copy(
            src_ref=values.at[pl.ds(own, CHUNK)], dst_ref=values.at[pl.ds(own, CHUNK)],
            send_sem=r.x_send.at[kind, k - 1], recv_sem=r.x_recv.at[kind, AUXES - 1 - k],
            device_id=(me, peers[k]), device_id_type=MESH,
        )

    def wait_summed(kind):
        into = r.high_in if kind == HIGH_SUM else r.low_in
        for k in range(1, AUXES):
            pltpu.make_async_remote_copy(
                src_ref=into.at[k - 1], dst_ref=into.at[k - 1],
                send_sem=r.x_send.at[kind, k - 1], recv_sem=r.x_recv.at[kind, k - 1],
                device_id=(me, peers[k]), device_id_type=MESH,
            ).wait_recv()

    def wait_spread(kind, k):
        values = r.high if kind == HIGH_ALL else r.low
        theirs = values.at[pl.ds(peers[k] * CHUNK, CHUNK)]
        pltpu.make_async_remote_copy(
            src_ref=theirs, dst_ref=theirs,
            send_sem=r.x_send.at[kind, k - 1], recv_sem=r.x_recv.at[kind, k - 1],
            device_id=(me, peers[k]), device_id_type=MESH,
        ).wait_recv()

    def halo(sweep, first, size, side):
        target = first + 2 * PAIRS if side == 0 else first
        return pltpu.make_async_remote_copy(
            src_ref=windows[sweep].at[pl.ds(PAIRS + first, size)],
            dst_ref=windows[sweep].at[pl.ds(target, size)],
            send_sem=r.halo_send.at[sweep, side], recv_sem=r.halo_recv.at[sweep, side],
            device_id=(left if side == 0 else right, ax), device_id_type=MESH,
        )

    def wait_halo(sweep):
        for side in range(2):
            done = pltpu.make_async_remote_copy(
                src_ref=windows[sweep].at[pl.ds(PAIRS, PAIRS)],
                dst_ref=windows[sweep].at[pl.ds(2 * PAIRS if side == 0 else 0, PAIRS)],
                send_sem=r.halo_send.at[sweep, side], recv_sem=r.halo_recv.at[sweep, side],
                device_id=(left if side == 0 else right, ax), device_id_type=MESH,
            )
            done.wait_send()
            done.wait_recv()

    for k in (2, 1, 3):

        def give(h, carry, k=k):
            for i in (2 * h, 2 * h + 1):
                values = part(peers[k] * CHUNK + i)
                top = values.astype(jnp.bfloat16)
                r.high_out[k - 1, i] = top
                r.low_out[k - 1, i] = (values - top.astype(jnp.float32)).astype(jnp.bfloat16)
            return carry

        lax.fori_loop(0, CHUNK // 2, give, 0)
        summed(HIGH_SUM, k).start()

    def keep(h, carry):
        for i in (2 * h, 2 * h + 1):
            r.own_part[i] = part(own + i)
        return carry

    lax.fori_loop(0, CHUNK // 2, keep, 0)
    wait_summed(HIGH_SUM)

    def add_high(i, carry):
        values = r.own_part[i]
        for k in range(AUXES - 1):
            values = values + r.high_in[k, i].astype(jnp.float32)
        r.high[own + i] = masked(own + i, values).astype(jnp.bfloat16)
        return carry

    lax.fori_loop(0, CHUNK, add_high, 0)
    for k in (2, 1, 3):
        spread(HIGH_ALL, k).start()

    def first_amplitudes(start):
        def body(i, carry):
            q = start + i
            windows[0][PAIRS + q] = (-r.high[q].astype(jnp.float32) * r.inverse[q]).astype(jnp.bfloat16)
            return carry

        lax.fori_loop(0, CHUNK, body, 0)
        for side in range(2):
            halo(0, start, CHUNK, side).start()

    first_amplitudes(own)
    for k in (2, 1, 3):
        summed(LOW_SUM, k).start()
    for k in (1, 3, 2):
        wait_spread(HIGH_ALL, k)
        first_amplitudes(pl.multiple_of(peers[k] * CHUNK, CHUNK))
    wait_summed(LOW_SUM)

    def add_low(i, carry):
        values = r.own_part[i]
        for k in range(AUXES - 1):
            values = values + r.high_in[k, i].astype(jnp.float32)
        for k in range(AUXES - 1):
            values = values + r.low_in[k, i].astype(jnp.float32)
        top = r.high[own + i].astype(jnp.float32)
        r.low[own + i] = (masked(own + i, values) - top).astype(jnp.bfloat16)
        return carry

    lax.fori_loop(0, CHUNK, add_low, 0)
    for k in (2, 1, 3):
        spread(LOW_ALL, k).start()

    for sweep in range(ITERS):
        wait_halo(sweep)
        if sweep == 0:
            for k in (1, 3, 2):
                wait_spread(LOW_ALL, k)

        def update(q, sweep=sweep):
            firsts = [
                jnp.dot(
                    r.weighted[q, :, n * TILE : (n + 1) * TILE],
                    windows[sweep][r.table[NEAR + q * 4 + n]],
                    preferred_element_type=jnp.float32,
                ).astype(jnp.bfloat16)
                for n in range(4)
            ]
            coupled = lax.dot_general(
                jnp.concatenate(firsts, axis=1), r.vecs[q], (((1,), (1,)), ((), ())),
                preferred_element_type=jnp.float32,
            )
            if sweep == 0:
                integrals = r.high[q].astype(jnp.float32) + r.low[q].astype(jnp.float32)
                r.integ[q] = integrals
            else:
                integrals = r.integ[q]
            current = (coupled - integrals) * r.inverse[q]
            if sweep < ITERS - 1:
                windows[sweep + 1][PAIRS + q] = current.astype(jnp.bfloat16)
            else:
                r.amp[q] = current
                r.pair_energy[q] = jnp.sum(integrals * (2.0 * current - current.T))

        def some(j, carry, sweep=sweep):
            for i in range(CHUNK):
                update(j * CHUNK + i)
            if sweep < ITERS - 1:
                for side in range(2):
                    halo(sweep + 1, pl.multiple_of(j * CHUNK, CHUNK), CHUNK, side).start()
            return carry

        lax.fori_loop(0, PAIRS // CHUNK, some, 0)

    for k in range(1, AUXES):
        for kind in (HIGH_SUM, LOW_SUM):
            summed(kind, k).wait_send()
        for kind in (HIGH_ALL, LOW_ALL):
            spread(kind, k).wait_send()


def run_kernel(exchanging, table, count, occ, source, coef, energy, coupling, inter):
    smem, vmem = pl.BlockSpec(memory_space=pltpu.SMEM), pl.BlockSpec(memory_space=pltpu.VMEM)
    hbm = pl.BlockSpec(memory_space=pl.ANY)
    scratch = dict(SCRATCH, **(EXCHANGE_SCRATCH if exchanging else {}))
    return pl.pallas_call(
        functools.partial(kernel, exchanging),
        out_shape=(
            jax.ShapeDtypeStruct((PAIRS, TILE, TILE), jnp.float32),
            jax.ShapeDtypeStruct((PAIRS,), jnp.float32),
        ),
        in_specs=[smem, smem, smem, vmem] + [hbm] * exchanging + [vmem, vmem, hbm],
        out_specs=(vmem, smem),
        scratch_shapes=[
            pltpu.SemaphoreType.DMA(v) if isinstance(v[0], int) else pltpu.VMEM(*v) for v in scratch.values()
        ],
        compiler_params=pltpu.CompilerParams(
            collective_id=0 if exchanging else 1, has_side_effects=True, vmem_limit_bytes=VMEM_LIMIT
        ),
    )(*([table, count, occ, source] + [coef] * exchanging + [energy, coupling, inter]))


def padded_exchange(blocks, coef, send_pos, own_source, own_rank):
    incoming = lax.all_to_all(
        blocks[send_pos], "pair", split_axis=0, concat_axis=0, tiled=True
    )
    arrived = incoming.reshape((OWNERS * CAP,) + blocks.shape[1:])[own_source * CAP + own_rank]
    arrived = arrived.reshape((PAIRS, 2, DOM) + blocks.shape[1:])
    coefs = coef.reshape(PAIRS, DOM, TILE, TILE)
    projected = jnp.einsum(
        "qmtxp,qtpn->qmxn", arrived, coefs, preferred_element_type=jnp.float32
    ).astype(jnp.bfloat16)
    return jnp.einsum(
        "qxa,qxb->qab", projected[:, 0], projected[:, 1], preferred_element_type=jnp.float32
    )


def route(source_dev, block_pos, me):
    plane, col = me // COLS, me % COLS
    both = (source_dev * BLOCKS + block_pos).reshape(OWNERS, TOTAL)
    source, position = both // BLOCKS, both % BLOCKS
    slots = jnp.arange(CAP, dtype=jnp.int32)
    devices = jnp.arange(OWNERS, dtype=jnp.int32)
    wanted = source == me
    ranking = jnp.cumsum(wanted.astype(jnp.int32), axis=1) - 1
    chosen = wanted[:, None, :] & (ranking[:, None, :] == slots[None, :, None])
    send_pos = jnp.sum(jnp.where(chosen, position[:, None, :], 0), axis=2)
    taken = jnp.sum((source[:, None, :] == devices[None, :, None]).astype(jnp.int32), axis=2)
    third = (taken > DIRECT).astype(jnp.int32)
    fits = jnp.max(jnp.sum(third.reshape(OWNERS, PLANES, COLS), axis=2)) <= EXTRA
    own_source = lax.dynamic_index_in_dim(source, me, 0, keepdims=False)
    order = jnp.arange(TOTAL, dtype=jnp.int32)
    earlier = (own_source[None, :] == own_source[:, None]) & (order[None, :] < order[:, None])
    own_rank = jnp.sum(earlier.astype(jnp.int32), axis=1)
    own_third = lax.dynamic_index_in_dim(third, me, 0, keepdims=False)
    before = (devices[None, :] < own_source[:, None]) & (
        devices[None, :] // COLS == own_source[:, None] // COLS
    )
    extra_rank = jnp.sum(jnp.where(before, own_third[None, :], 0), axis=1)
    extra_row = (
        DIRECT * OWNERS
        + lax.rem(own_source // COLS - plane + PLANES, PLANES) * EXTRA
        + jnp.minimum(extra_rank, EXTRA - 1)
    )
    direct_row = lax.rem(own_source - me + OWNERS, OWNERS) * DIRECT + own_rank
    land_row = jnp.where(own_rank >= DIRECT, extra_row, direct_row)
    column = lax.dynamic_index_in_dim(third.reshape(PLANES, COLS, PLANES, COLS), col, 1, keepdims=False)
    column = lax.dynamic_index_in_dim(column, plane, 1, keepdims=False)
    cols = jnp.arange(COLS, dtype=jnp.int32)
    place = jnp.cumsum(column, axis=1) - column
    hit = (column == 1)[:, None, :] & (place[:, None, :] == jnp.arange(EXTRA)[None, :, None])
    back = lax.rem(cols - col + COLS, COLS)
    relay_row = jnp.sum(jnp.where(hit, back[None, None, :], 0), axis=2) * PLANES + cols[:, None]
    return send_pos, relay_row, land_row, own_source, own_rank, fits


def shards(
    blocks, pno_coef, source_dev, block_pos, pno_energy, occ_energy, pno_count, neighbour, coupling, intersection,
):
    me = lax.axis_index("pair")
    send_pos, relay_row, land_row, own_source, own_rank, fits = route(source_dev, block_pos, me)
    near = neighbour - (me - 1) * PAIRS
    table = jnp.concatenate([a.reshape(-1) for a in (send_pos, relay_row, land_row, near)])

    def finish(exchanging, source):
        return run_kernel(
            exchanging, table, pno_count, occ_energy, source, pno_coef, pno_energy, coupling, intersection
        )

    return lax.cond(
        fits,
        lambda: finish(True, blocks),
        lambda: finish(False, padded_exchange(blocks, pno_coef, send_pos, own_source, own_rank)),
    )


def solution(mesh):
    return jax.shard_map(
        shards,
        mesh=mesh,
        in_specs=(
            P("pair", "aux", None),
            P("pair", None, None),
            P(),
            P(),
            P("pair", None),
            P("pair"),
            P("pair"),
            P("pair", None),
            P("pair", None),
            P("pair", None, None, None),
        ),
        out_specs=(P("pair", None, None), P("pair")),
        check_vma=False,
    )
```

time: 405 us -> 181 us (0.45)
  waiting for transfers between devices: 233 us -> 0 us
  Pallas kernels: 0 us -> 168 us
  matrix products: 68.6 us -> 0 us
  local copies, waits for them, and re-layouts: 38.8 us -> 4.09 us
  starting transfers between devices: 28.7 us -> 0 us
  between operations: 14.4 us -> 1.45 us
  other arithmetic: 17.1 us -> 4.49 us
    pallas_call x0 -> x1, Pallas kernels: none -> 168 us  [run_kernel(): pl.pallas_call(functools.partial(kernel, exchanging), out_shape=(jax.Shap...]
    all_to_all x1 -> x0, waiting for transfers between devices: 139 us -> none  [shards(): lax.all_to_all(outgoing, 'pair', split_axis=0, concat_axis=0, tiled=True)]
    dot_general x8 -> x0, matrix products: 68.6 us -> none  [the longest x3 36 us: couple_rows(): first = jnp.einsum('gnab,gnbc->gnac', intersections, near, precision=HIGH)]
    psum x1 -> x0, waiting for transfers between devices: 47.4 us -> none  [shards(): integrals = mask * lax.psum(partial_ints, 'aux')]
    ppermute x6 -> x0, waiting for transfers between devices: 47.1 us -> none  [the longest x3 27.4 us: with_halo(): lax.ppermute(tail, axis, [(i, (i + 1) % count) for i in range(ends)])]
    gather x5 -> x0, local copies, waits for them, and re-layouts: 27.9 us -> none  [the longest x3 13.9 us: couple_rows(): near = window[near_index]]
    ppermute x6 -> x0, starting transfers between devices: 16.3 us -> none  [the longest x3 8.89 us: with_halo(): lax.ppermute(tail, axis, [(i, (i + 1) % count) for i in range(ends)])]
    all_to_all x1 -> x0, starting transfers between devices: 12.4 us -> none  [shards(): lax.all_to_all(outgoing, 'pair', split_axis=0, concat_axis=0, tiled=True)]
  transfers between devices with their start and end apart: 8 -> 0, of which waited for: 8 -> 0; matrix products, arithmetic and copies ran while one was open for 0% -> 0% of each run, Pallas kernels for 0% -> 0%
where the time goes in v2:
time: 181 us; the launch traced here: 178 us
  Pallas kernels  168 us (93%)
  other arithmetic  4.49 us (2%)
  local copies, waits for them, and re-layouts  4.09 us (2%)
    pallas_call x1, Pallas kernels, run_kernel(): pl.pallas_call(functools.partial(kernel, exchanging), out_shape=(jax.Shap...  168 us

profile of v2, /device:TPU:25, one launch (start us, length us, event | category | flops | bytes accessed | tf_op | source)
XLA Modules:
  0.0 178.3 jit_solution(14088124249883936445)
XLA Ops:
  0.7 0.8 multiply_add_fusion
  1.5 0.2 copy.40
  1.7 0.3 reshape.263
  1.9 1.2 convert_reduce_fusion
  3.1 0.1 reshape.267
  3.3 0.2 reduce_window_sum.23
  3.4 0.1 select_reduce_fusion.2
  3.6 0.1 copy.43
  3.7 0.1 add.122
  3.8 0.1 select_reduce_fusion.1
  3.9 0.2 convert_reduce_fusion.1
  4.1 0.3 reduce_window_sum.22
  4.4 0.1 select_reduce_fusion
  4.6 0.1 copy.42
  4.7 0.1 reshape.264
  4.8 0.7 broadcast_subtract_fusion
  5.5 0.1 copy.44
  5.6 0.1 reshape.265
  5.7 0.1 pad_add_fusion
  5.8 0.1 copy.41
  5.9 0.6 reduce_max.9
  7.2 169.7 %conditional.1 = ((f32[16,128,128]{2,1,0:T(8,128)S(1)}, f32[16]{0:T(128)S(1)})) conditional(s32[]{:T(128)} %convert_element_type.37, (s32[64,3]{0,1:T(4,128)S(1)}, bf16[64,128,128]{2,1,0:T(8,128)(2,1)}, s32[128]{0:T(128)S(1)}, s32[128]{0:T(128)S(1)}, bf16[16,512,128]{2,1,0:T(8,128)(2,1)}, /*index=5*/s32[400]{0:T(512)S(1)}, s32[16]{0:T(128)}, ...), branch_computations={%region_9.10_spmd, %region_10.11_spmd} | conditional | flops 604507328 | bytes 74500816 | solution.py:507
  7.4 1.4 copy.47.refs_6_
  8.7 168.1 %branch_1_fun.1 = (f32[16,128,128]{2,1,0:T(8,128)S(1)}, f32[16]{0:T(128)S(1)}) custom-call(s32[400]{0:T(512)S(1)} %get-tuple-element.49.refs_0_, s32[16]{0:T(128)} %get-tuple-element.50.refs_1_, f32[16]{0:T(128)} %get-tuple-element.51.refs_2_, bf16[64,128,128]{2,1,0:T(8,128)(2,1)} %get-tuple-element.52.refs_3_, ...), custom_call_target="tpu_custom_call" | custom-call | tf_op jit(solution)/shard_map/cond/branch_1_fun/pallas_call | solution.py:423
  176.8 1.0 copy.57
  177.8 0.5 copy.58
  (13 shorter events, 0.2 us)

commit v3 on v2

--- a/solution.py
+++ b/solution.py
@@ -23,7 +23,7 @@
 TILE = 128
 CAP = 3
 DIRECT = 2
-EXTRA = 2
+EXTRAS = (1, 2)
 
 VMEM_LIMIT = 56 * 2**20
 CHUNK = PAIRS // AUXES
@@ -50,35 +50,38 @@
     "integ": ((PAIRS, TILE, TILE), jnp.float32),
     "inverse": ((PAIRS, TILE, TILE), jnp.float32),
     "own_part": ((CHUNK, TILE, TILE), jnp.float32),
-    "high_out": ((AUXES - 1, CHUNK, TILE, TILE), jnp.bfloat16),
-    "low_out": ((AUXES - 1, CHUNK, TILE, TILE), jnp.bfloat16),
-    "high_in": ((AUXES - 1, CHUNK, TILE, TILE), jnp.bfloat16),
-    "low_in": ((AUXES - 1, CHUNK, TILE, TILE), jnp.bfloat16),
+    "share_out": ((AUXES - 1, CHUNK, TILE, TILE), jnp.bfloat16),
+    "share_in": ((AUXES - 1, CHUNK, TILE, TILE), jnp.bfloat16),
     "high": ((PAIRS, TILE, TILE), jnp.bfloat16),
     "low": ((PAIRS, TILE, TILE), jnp.bfloat16),
     "local_sem": (2,),
-    "x_send": (4, AUXES - 1),
-    "x_recv": (4, AUXES - 1),
+    "x_send": (3, AUXES - 1),
+    "x_recv": (3, AUXES - 1),
     "halo_send": (ITERS, 2),
     "halo_recv": (ITERS, 2),
 }
-EXCHANGE_SCRATCH = {
-    "coef": ((PAIRS, DOM * TILE, TILE), jnp.bfloat16),
-    "outgoing": ((DIRECT * OWNERS, TILE, TILE), jnp.bfloat16),
-    "landing": ((DIRECT * OWNERS + EXTRA * PLANES, TILE, TILE), jnp.bfloat16),
-    "relay_out": ((OWNERS, TILE, TILE), jnp.bfloat16),
-    "relay_in": ((OWNERS, TILE, TILE), jnp.bfloat16),
-    "extra_out": ((EXTRA * PLANES, TILE, TILE), jnp.bfloat16),
-    "block_sem": (6,),
-}
-SEND, RELAY, LAND = 0, OWNERS * CAP, OWNERS * CAP + PLANES * EXTRA
-NEAR = LAND + TOTAL
-HIGH_SUM, HIGH_ALL, LOW_SUM, LOW_ALL = range(4)
-
-
-def kernel(exchanging, *refs):
-    names = ["table", "count", "occ", "source", "coef_hbm", "energy", "coupling", "inter_hbm", "amp", "pair_energy"]
-    names += list(SCRATCH) + (list(EXCHANGE_SCRATCH) if exchanging else [])
+
+
+def exchange_scratch(extra):
+    return {
+        "coef": ((PAIRS, DOM * TILE, TILE), jnp.bfloat16),
+        "outgoing": ((DIRECT * OWNERS, TILE, TILE), jnp.bfloat16),
+        "landing": ((DIRECT * OWNERS + extra * PLANES, TILE, TILE), jnp.bfloat16),
+        "relay_out": ((OWNERS, TILE, TILE), jnp.bfloat16),
+        "relay_in": ((OWNERS, TILE, TILE), jnp.bfloat16),
+        "extra_out": ((extra * PLANES, TILE, TILE), jnp.bfloat16),
+        "block_sem": (6,),
+    }
+
+
+SEND, RELAY, LAND = 0, OWNERS * CAP, OWNERS * CAP + PLANES * max(EXTRAS)
+SUM, HIGH, LOW = range(3)
+
+
+def kernel(extra, *refs):
+    exchanging = extra > 0
+    names = ["table", "count", "occ", "source", "coef_hbm", "energy", "near", "coupling", "inter_hbm", "amp", "pair_energy"]
+    names += list(SCRATCH) + (list(exchange_scratch(extra)) if exchanging else [])
     if not exchanging:
         names.remove("coef_hbm")
     r = types.SimpleNamespace(**dict(zip(names, refs, strict=True)))
@@ -130,7 +133,7 @@
                 v = r.inter[q, n]
                 cut = slice(n * TILE, (n + 1) * TILE)
                 r.vecs[q, :, cut] = v.astype(jnp.bfloat16)
-                r.weighted[q, :, cut] = (v * r.coupling[pl.ds(q, 1), n : n + 1]).astype(jnp.bfloat16)
+                r.weighted[q, :, cut] = (v * r.coupling[n, q]).astype(jnp.bfloat16)
             return carry
 
         lax.fori_loop(0, PAIRS, narrow, 0)
@@ -183,8 +186,8 @@
 
         def from_relay(k):
             return pltpu.make_async_remote_copy(
-                src_ref=r.extra_out.at[pl.ds(EXTRA * k, EXTRA)],
-                dst_ref=landing.at[pl.ds(DIRECT * OWNERS + EXTRA * (PLANES - k), EXTRA)],
+                src_ref=r.extra_out.at[pl.ds(extra * k, extra)],
+                dst_ref=landing.at[pl.ds(DIRECT * OWNERS + extra * (PLANES - k), extra)],
                 send_sem=r.block_sem.at[4], recv_sem=r.block_sem.at[5],
                 device_id=(lax.rem(plane + k, PLANES) * COLS + col, ax), device_id_type=MESH,
             )
@@ -204,12 +207,12 @@
         relayed.wait_recv()
         for k in (4, 3, 5, 2, 6, 1, 7, 0):
             b = lax.rem(plane + k, PLANES)
-            for e in range(EXTRA):
-                block = r.relay_in[r.table[RELAY + b * EXTRA + e]]
+            for e in range(extra):
+                block = r.relay_in[r.table[RELAY + b * max(EXTRAS) + e]]
                 if k == 0:
                     landing[DIRECT * OWNERS + e] = block
                 else:
-                    r.extra_out[EXTRA * k + e] = block
+                    r.extra_out[extra * k + e] = block
             if k != 0:
                 from_relay(k).start()
 
@@ -219,8 +222,8 @@
         sent.wait_send()
         sent.wait_recv()
         extras = pltpu.make_async_remote_copy(
-            src_ref=r.extra_out.at[pl.ds(EXTRA, EXTRA * (PLANES - 1))],
-            dst_ref=landing.at[pl.ds(DIRECT * OWNERS + EXTRA, EXTRA * (PLANES - 1))],
+            src_ref=r.extra_out.at[pl.ds(extra, extra * (PLANES - 1))],
+            dst_ref=landing.at[pl.ds(DIRECT * OWNERS + extra, extra * (PLANES - 1))],
             send_sem=r.block_sem.at[4], recv_sem=r.block_sem.at[5],
             device_id=(right, ax), device_id_type=MESH,
         )
@@ -250,33 +253,31 @@
         def part(q):
             return r.source[q]
 
-    def summed(kind, k):
-        out, into = (r.high_out, r.high_in) if kind == HIGH_SUM else (r.low_out, r.low_in)
+    def share(k):
         return pltpu.make_async_remote_copy(
-            src_ref=out.at[k - 1], dst_ref=into.at[AUXES - 1 - k],
-            send_sem=r.x_send.at[kind, k - 1], recv_sem=r.x_recv.at[kind, AUXES - 1 - k],
+            src_ref=r.share_out.at[k - 1], dst_ref=r.share_in.at[AUXES - 1 - k],
+            send_sem=r.x_send.at[SUM, k - 1], recv_sem=r.x_recv.at[SUM, AUXES - 1 - k],
             device_id=(me, peers[k]), device_id_type=MESH,
         )
 
     def spread(kind, k):
-        values = r.high if kind == HIGH_ALL else r.low
+        values = r.high if kind == HIGH else r.low
         return pltpu.make_async_remote_copy(
             src_ref=values.at[pl.ds(own, CHUNK)], dst_ref=values.at[pl.ds(own, CHUNK)],
             send_sem=r.x_send.at[kind, k - 1], recv_sem=r.x_recv.at[kind, AUXES - 1 - k],
             device_id=(me, peers[k]), device_id_type=MESH,
         )
 
-    def wait_summed(kind):
-        into = r.high_in if kind == HIGH_SUM else r.low_in
+    def wait_shares():
         for k in range(1, AUXES):
             pltpu.make_async_remote_copy(
-                src_ref=into.at[k - 1], dst_ref=into.at[k - 1],
-                send_sem=r.x_send.at[kind, k - 1], recv_sem=r.x_recv.at[kind, k - 1],
+                src_ref=r.share_in.at[k - 1], dst_ref=r.share_in.at[k - 1],
+                send_sem=r.x_send.at[SUM, k - 1], recv_sem=r.x_recv.at[SUM, k - 1],
                 device_id=(me, peers[k]), device_id_type=MESH,
             ).wait_recv()
 
     def wait_spread(kind, k):
-        values = r.high if kind == HIGH_ALL else r.low
+        values = r.high if kind == HIGH else r.low
         theirs = values.at[pl.ds(peers[k] * CHUNK, CHUNK)]
         pltpu.make_async_remote_copy(
             src_ref=theirs, dst_ref=theirs,
@@ -305,36 +306,27 @@
             done.wait_recv()
 
     for k in (2, 1, 3):
-
-        def give(h, carry, k=k):
-            for i in (2 * h, 2 * h + 1):
-                values = part(peers[k] * CHUNK + i)
-                top = values.astype(jnp.bfloat16)
-                r.high_out[k - 1, i] = top
-                r.low_out[k - 1, i] = (values - top.astype(jnp.float32)).astype(jnp.bfloat16)
-            return carry
-
-        lax.fori_loop(0, CHUNK // 2, give, 0)
-        summed(HIGH_SUM, k).start()
-
-    def keep(h, carry):
-        for i in (2 * h, 2 * h + 1):
-            r.own_part[i] = part(own + i)
-        return carry
-
-    lax.fori_loop(0, CHUNK // 2, keep, 0)
-    wait_summed(HIGH_SUM)
-
-    def add_high(i, carry):
+        for i in range(CHUNK):
+            r.share_out[k - 1, i] = part(peers[k] * CHUNK + i).astype(jnp.bfloat16)
+        share(k).start()
+    for i in range(CHUNK):
+        r.own_part[i] = part(own + i)
+    wait_shares()
+
+    def add(i, carry):
         values = r.own_part[i]
         for k in range(AUXES - 1):
-            values = values + r.high_in[k, i].astype(jnp.float32)
-        r.high[own + i] = masked(own + i, values).astype(jnp.bfloat16)
+            values = values + r.share_in[k, i].astype(jnp.float32)
+        values = masked(own + i, values)
+        top = values.astype(jnp.bfloat16)
+        r.high[own + i] = top
+        r.low[own + i] = (values - top.astype(jnp.float32)).astype(jnp.bfloat16)
         return carry
 
-    lax.fori_loop(0, CHUNK, add_high, 0)
-    for k in (2, 1, 3):
-        spread(HIGH_ALL, k).start()
+    lax.fori_loop(0, CHUNK, add, 0)
+    for kind in (HIGH, LOW):
+        for k in (2, 1, 3):
+            spread(kind, k).start()
 
     def first_amplitudes(start):
         def body(i, carry):
@@ -347,38 +339,21 @@
             halo(0, start, CHUNK, side).start()
 
     first_amplitudes(own)
-    for k in (2, 1, 3):
-        summed(LOW_SUM, k).start()
     for k in (1, 3, 2):
-        wait_spread(HIGH_ALL, k)
+        wait_spread(HIGH, k)
         first_amplitudes(pl.multiple_of(peers[k] * CHUNK, CHUNK))
-    wait_summed(LOW_SUM)
-
-    def add_low(i, carry):
-        values = r.own_part[i]
-        for k in range(AUXES - 1):
-            values = values + r.high_in[k, i].astype(jnp.float32)
-        for k in range(AUXES - 1):
-            values = values + r.low_in[k, i].astype(jnp.float32)
-        top = r.high[own + i].astype(jnp.float32)
-        r.low[own + i] = (masked(own + i, values) - top).astype(jnp.bfloat16)
-        return carry
-
-    lax.fori_loop(0, CHUNK, add_low, 0)
-    for k in (2, 1, 3):
-        spread(LOW_ALL, k).start()
 
     for sweep in range(ITERS):
         wait_halo(sweep)
         if sweep == 0:
             for k in (1, 3, 2):
-                wait_spread(LOW_ALL, k)
+                wait_spread(LOW, k)
 
         def update(q, sweep=sweep):
             firsts = [
                 jnp.dot(
                     r.weighted[q, :, n * TILE : (n + 1) * TILE],
-                    windows[sweep][r.table[NEAR + q * 4 + n]],
+                    windows[sweep][jnp.clip(r.near[n, q] - (me - 1) * PAIRS, 0, 3 * PAIRS - 1)],
                     preferred_element_type=jnp.float32,
                 ).astype(jnp.bfloat16)
                 for n in range(4)
@@ -410,31 +385,31 @@
         lax.fori_loop(0, PAIRS // CHUNK, some, 0)
 
     for k in range(1, AUXES):
-        for kind in (HIGH_SUM, LOW_SUM):
-            summed(kind, k).wait_send()
-        for kind in (HIGH_ALL, LOW_ALL):
+        share(k).wait_send()
+        for kind in (HIGH, LOW):
             spread(kind, k).wait_send()
 
 
-def run_kernel(exchanging, table, count, occ, source, coef, energy, coupling, inter):
+def run_kernel(extra, table, count, occ, source, coef, energy, near, coupling, inter):
+    exchanging = extra > 0
     smem, vmem = pl.BlockSpec(memory_space=pltpu.SMEM), pl.BlockSpec(memory_space=pltpu.VMEM)
     hbm = pl.BlockSpec(memory_space=pl.ANY)
-    scratch = dict(SCRATCH, **(EXCHANGE_SCRATCH if exchanging else {}))
+    scratch = dict(SCRATCH, **(exchange_scratch(extra) if exchanging else {}))
     return pl.pallas_call(
-        functools.partial(kernel, exchanging),
+        functools.partial(kernel, extra),
         out_shape=(
             jax.ShapeDtypeStruct((PAIRS, TILE, TILE), jnp.float32),
             jax.ShapeDtypeStruct((PAIRS,), jnp.float32),
         ),
-        in_specs=[smem, smem, smem, vmem] + [hbm] * exchanging + [vmem, vmem, hbm],
+        in_specs=[smem, smem, smem, vmem] + [hbm] * exchanging + [vmem, smem, smem, hbm],
         out_specs=(vmem, smem),
         scratch_shapes=[
             pltpu.SemaphoreType.DMA(v) if isinstance(v[0], int) else pltpu.VMEM(*v) for v in scratch.values()
         ],
         compiler_params=pltpu.CompilerParams(
-            collective_id=0 if exchanging else 1, has_side_effects=True, vmem_limit_bytes=VMEM_LIMIT
+            collective_id=extra, has_side_effects=True, vmem_limit_bytes=VMEM_LIMIT
         ),
-    )(*([table, count, occ, source] + [coef] * exchanging + [energy, coupling, inter]))
+    )(*([table, count, occ, source] + [coef] * exchanging + [energy, near, coupling, inter]))
 
 
 def padded_exchange(blocks, coef, send_pos, own_source, own_rank):
@@ -464,7 +439,8 @@
     send_pos = jnp.sum(jnp.where(chosen, position[:, None, :], 0), axis=2)
     taken = jnp.sum((source[:, None, :] == devices[None, :, None]).astype(jnp.int32), axis=2)
     third = (taken > DIRECT).astype(jnp.int32)
-    fits = jnp.max(jnp.sum(third.reshape(OWNERS, PLANES, COLS), axis=2)) <= EXTRA
+    most = jnp.max(jnp.sum(third.reshape(OWNERS, PLANES, COLS), axis=2))
+    room = jnp.minimum(jnp.maximum(most, EXTRAS[0]), EXTRAS[1])
     own_source = lax.dynamic_index_in_dim(source, me, 0, keepdims=False)
     order = jnp.arange(TOTAL, dtype=jnp.int32)
     earlier = (own_source[None, :] == own_source[:, None]) & (order[None, :] < order[:, None])
@@ -476,8 +452,8 @@
     extra_rank = jnp.sum(jnp.where(before, own_third[None, :], 0), axis=1)
     extra_row = (
         DIRECT * OWNERS
-        + lax.rem(own_source // COLS - plane + PLANES, PLANES) * EXTRA
-        + jnp.minimum(extra_rank, EXTRA - 1)
+        + lax.rem(own_source // COLS - plane + PLANES, PLANES) * room
+        + jnp.minimum(extra_rank, room - 1)
     )
     direct_row = lax.rem(own_source - me + OWNERS, OWNERS) * DIRECT + own_rank
     land_row = jnp.where(own_rank >= DIRECT, extra_row, direct_row)
@@ -485,29 +461,31 @@
     column = lax.dynamic_index_in_dim(column, plane, 1, keepdims=False)
     cols = jnp.arange(COLS, dtype=jnp.int32)
     place = jnp.cumsum(column, axis=1) - column
-    hit = (column == 1)[:, None, :] & (place[:, None, :] == jnp.arange(EXTRA)[None, :, None])
+    hit = (column == 1)[:, None, :] & (place[:, None, :] == jnp.arange(EXTRAS[1])[None, :, None])
     back = lax.rem(cols - col + COLS, COLS)
     relay_row = jnp.sum(jnp.where(hit, back[None, None, :], 0), axis=2) * PLANES + cols[:, None]
-    return send_pos, relay_row, land_row, own_source, own_rank, fits
+    return send_pos, relay_row, land_row, own_source, own_rank, most
 
 
 def shards(
     blocks, pno_coef, source_dev, block_pos, pno_energy, occ_energy, pno_count, neighbour, coupling, intersection,
 ):
     me = lax.axis_index("pair")
-    send_pos, relay_row, land_row, own_source, own_rank, fits = route(source_dev, block_pos, me)
-    near = neighbour - (me - 1) * PAIRS
-    table = jnp.concatenate([a.reshape(-1) for a in (send_pos, relay_row, land_row, near)])
-
-    def finish(exchanging, source):
+    send_pos, relay_row, land_row, own_source, own_rank, most = route(source_dev, block_pos, me)
+    table = jnp.concatenate([a.reshape(-1) for a in (send_pos, relay_row, land_row)])
+
+    def finish(extra, source):
         return run_kernel(
-            exchanging, table, pno_count, occ_energy, source, pno_coef, pno_energy, coupling, intersection
+            extra, table, pno_count, occ_energy, source, pno_coef, pno_energy, neighbour.T, coupling.T, intersection
         )
 
-    return lax.cond(
-        fits,
-        lambda: finish(True, blocks),
-        lambda: finish(False, padded_exchange(blocks, pno_coef, send_pos, own_source, own_rank)),
+    return lax.switch(
+        jnp.clip(most, 1, 3) - 1,
+        [
+            lambda: finish(1, blocks),
+            lambda: finish(2, blocks),
+            lambda: finish(0, padded_exchange(blocks, pno_coef, send_pos, own_source, own_rank)),
+        ],
     )
 
 

time: 181 us -> 174 us (0.961)
  Pallas kernels: 168 us -> 164 us
    pallas_call x1, Pallas kernels: 168 us -> 164 us  [run_kernel(): pl.pallas_call(functools.partial(kernel, extra), out_shape=(jax.ShapeDtyp...]
where the time goes in v3:
time: 174 us; the launch traced here: 172 us
  Pallas kernels  164 us (94%)
  other arithmetic  3.81 us (2%)
  local copies, waits for them, and re-layouts  2.56 us (1%)
    pallas_call x1, Pallas kernels, run_kernel(): pl.pallas_call(functools.partial(kernel, extra), out_shape=(jax.ShapeDtyp...  164 us

profile of v3, /device:TPU:25, one launch (start us, length us, event | category | flops | bytes accessed | tf_op | source)
XLA Modules:
  0.0 171.7 jit_solution(2669104933536612343)
XLA Ops:
  0.7 0.8 multiply_add_fusion
  1.5 0.2 copy.30
  1.7 0.3 reshape.260
  1.9 1.2 convert_reduce_fusion
  3.1 0.1 reshape.263
  3.3 0.2 reduce_window_sum.23
  3.4 0.1 select_reduce_fusion.2
  3.6 0.1 copy.33
  3.7 0.1 add.122
  3.8 0.1 select_reduce_fusion.1
  3.9 0.2 convert_reduce_fusion.1
  4.1 0.1 copy.31
  4.2 0.6 reduce_max.9
  5.5 0.3 reduce_window_sum.22
  5.8 0.1 select_reduce_fusion
  6.0 0.1 copy.32
  6.1 0.1 reshape.261
  6.2 0.1 pad_add_fusion
  6.3 163.9 %conditional.1 = ((f32[16,128,128]{2,1,0:T(8,128)S(1)}, f32[16]{0:T(128)S(1)})) conditional(s32[]{:T(128)} %clamp.11, (s32[16,4]{0,1:T(4,128)}, f32[16,4]{0,1:T(4,128)}, s32[336]{0:T(512)S(1)}, s32[16]{0:T(128)}, f32[16]{0:T(128)}, /*index=5*/bf16[64,128,128]{2,1,0:T(8,128)(2,1)}, bf16[16,512,128]{2,1,0:T(8,128)(2,1)}, ...), branch_computations={%region_9.10_spmd, %region_10.11_spmd, %region_11.12_spmd} | conditional | flops 604507328 | bytes 74501360 | solution.py:482
  6.5 163.5 %branch_1_fun.1 = (f32[16,128,128]{2,1,0:T(8,128)S(1)}, f32[16]{0:T(128)S(1)}) custom-call(s32[336]{0:T(512)S(1)} %get-tuple-element.69.refs_0_, s32[16]{0:T(128)} %get-tuple-element.70.refs_1_, f32[16]{0:T(128)} %get-tuple-element.71.refs_2_, bf16[64,128,128]{2,1,0:T(8,128)(2,1)} %get-tuple-element.72.refs_3_, ...), custom_call_target="tpu_custom_call" | custom-call | tf_op jit(solution)/shard_map/cond/branch_1_fun/pallas_call | solution.py:398
  170.2 1.0 copy.46
  171.2 0.5 copy.47
  (13 shorter events, 0.2 us)

commit v4 on v3

--- a/solution.py
+++ b/solution.py
@@ -47,8 +47,9 @@
     "window0": ((3 * PAIRS, TILE, TILE), jnp.bfloat16),
     "window1": ((3 * PAIRS, TILE, TILE), jnp.bfloat16),
     "window2": ((3 * PAIRS, TILE, TILE), jnp.bfloat16),
+    "inverse": ((PAIRS, TILE, TILE), jnp.float32),
     "integ": ((PAIRS, TILE, TILE), jnp.float32),
-    "inverse": ((PAIRS, TILE, TILE), jnp.float32),
+    "factor": ((PAIRS, TILE, TILE), jnp.float32),
     "own_part": ((CHUNK, TILE, TILE), jnp.float32),
     "share_out": ((AUXES - 1, CHUNK, TILE, TILE), jnp.bfloat16),
     "share_in": ((AUXES - 1, CHUNK, TILE, TILE), jnp.bfloat16),
@@ -324,9 +325,8 @@
         return carry
 
     lax.fori_loop(0, CHUNK, add, 0)
-    for kind in (HIGH, LOW):
-        for k in (2, 1, 3):
-            spread(kind, k).start()
+    for k in (2, 1, 3):
+        spread(HIGH, k).start()
 
     def first_amplitudes(start):
         def body(i, carry):
@@ -342,12 +342,21 @@
     for k in (1, 3, 2):
         wait_spread(HIGH, k)
         first_amplitudes(pl.multiple_of(peers[k] * CHUNK, CHUNK))
+    for k in (2, 1, 3):
+        spread(LOW, k).start()
+
+    def both_halves(q, carry):
+        integrals = r.high[q].astype(jnp.float32) + r.low[q].astype(jnp.float32)
+        r.integ[q] = integrals
+        r.factor[q] = 2.0 * integrals - integrals.T
+        return carry
 
     for sweep in range(ITERS):
-        wait_halo(sweep)
-        if sweep == 0:
+        if sweep == ITERS - 1:
             for k in (1, 3, 2):
                 wait_spread(LOW, k)
+            lax.fori_loop(0, PAIRS, both_halves, 0)
+        wait_halo(sweep)
 
         def update(q, sweep=sweep):
             firsts = [
@@ -362,17 +371,13 @@
                 jnp.concatenate(firsts, axis=1), r.vecs[q], (((1,), (1,)), ((), ())),
                 preferred_element_type=jnp.float32,
             )
-            if sweep == 0:
-                integrals = r.high[q].astype(jnp.float32) + r.low[q].astype(jnp.float32)
-                r.integ[q] = integrals
-            else:
-                integrals = r.integ[q]
+            integrals = r.high[q].astype(jnp.float32) if sweep < ITERS - 1 else r.integ[q]
             current = (coupled - integrals) * r.inverse[q]
             if sweep < ITERS - 1:
                 windows[sweep + 1][PAIRS + q] = current.astype(jnp.bfloat16)
             else:
                 r.amp[q] = current
-                r.pair_energy[q] = jnp.sum(integrals * (2.0 * current - current.T))
+                r.pair_energy[q] = jnp.sum(r.factor[q] * current)
 
         def some(j, carry, sweep=sweep):
             for i in range(CHUNK):

time: 174 us -> 167 us (0.960)
  Pallas kernels: 164 us -> 156 us
    pallas_call x1, Pallas kernels: 164 us -> 156 us  [run_kernel(): pl.pallas_call(functools.partial(kernel, extra), out_shape=(jax.ShapeDtyp...]
where the time goes in v4:
time: 167 us; the launch traced here: 164 us
  Pallas kernels  156 us (93%)
  other arithmetic  3.81 us (2%)
  local copies, waits for them, and re-layouts  2.56 us (2%)
    pallas_call x1, Pallas kernels, run_kernel(): pl.pallas_call(functools.partial(kernel, extra), out_shape=(jax.ShapeDtyp...  156 us

profile of v4, /device:TPU:25, one launch (start us, length us, event | category | flops | bytes accessed | tf_op | source)
XLA Modules:
  0.0 164.2 jit_solution(14894121901627135258)
XLA Ops:
  0.7 0.8 multiply_add_fusion
  1.5 0.2 copy.30
  1.7 0.3 reshape.260
  1.9 1.2 convert_reduce_fusion
  3.1 0.1 reshape.263
  3.3 0.2 reduce_window_sum.23
  3.4 0.1 select_reduce_fusion.2
  3.6 0.1 copy.33
  3.7 0.1 add.122
  3.8 0.1 select_reduce_fusion.1
  3.9 0.2 convert_reduce_fusion.1
  4.1 0.1 copy.31
  4.2 0.6 reduce_max.9
  5.5 0.3 reduce_window_sum.22
  5.8 0.1 select_reduce_fusion
  6.0 0.1 copy.32
  6.1 0.1 reshape.261
  6.2 0.1 pad_add_fusion
  6.3 156.4 %conditional.1 = ((f32[16,128,128]{2,1,0:T(8,128)S(1)}, f32[16]{0:T(128)S(1)})) conditional(s32[]{:T(128)} %clamp.11, (s32[16,4]{0,1:T(4,128)}, f32[16,4]{0,1:T(4,128)}, s32[336]{0:T(512)S(1)}, s32[16]{0:T(128)}, f32[16]{0:T(128)}, /*index=5*/bf16[64,128,128]{2,1,0:T(8,128)(2,1)}, bf16[16,512,128]{2,1,0:T(8,128)(2,1)}, ...), branch_computations={%region_9.10_spmd, %region_10.11_spmd, %region_11.12_spmd} | conditional | flops 604507328 | bytes 74501360 | solution.py:487
  6.3 156.1 %branch_0_fun.1 = (f32[16,128,128]{2,1,0:T(8,128)S(1)}, f32[16]{0:T(128)S(1)}) custom-call(s32[336]{0:T(512)S(1)} %get-tuple-element.60.refs_0_, s32[16]{0:T(128)} %get-tuple-element.61.refs_1_, f32[16]{0:T(128)} %get-tuple-element.62.refs_2_, bf16[64,128,128]{2,1,0:T(8,128)(2,1)} %get-tuple-element.63.refs_3_, ...), custom_call_target="tpu_custom_call" | custom-call | tf_op jit(solution)/shard_map/cond/branch_0_fun/pallas_call | solution.py:403
  162.7 1.0 copy.46
  163.7 0.5 copy.47
  (13 shorter events, 0.2 us)

commit v5 on v4

--- a/solution.py
+++ b/solution.py
@@ -75,7 +75,10 @@
     }
 
 
-SEND, RELAY, LAND = 0, OWNERS * CAP, OWNERS * CAP + PLANES * max(EXTRAS)
+SEND = 0
+RELAY = SEND + CAP * PLANES
+LAND = RELAY + max(EXTRAS) * PLANES
+ROWS = LAND + REQ
 SUM, HIGH, LOW = range(3)
 
 
@@ -145,13 +148,12 @@
         def fill(k, carry):
             dst = lax.rem(me + k, OWNERS)
             for s in range(DIRECT):
-                outgoing[DIRECT * k + s] = blocks[r.table[SEND + dst * CAP + s]]
+                outgoing[DIRECT * k + s] = blocks[r.table[SEND + s * PLANES + dst // COLS, dst % COLS]]
             return carry
 
         def fill_relay(i, carry):
             k, b = i // PLANES, i % PLANES
-            dst = b * COLS + lax.rem(col + k, COLS)
-            r.relay_out[i] = blocks[r.table[SEND + dst * CAP + DIRECT]]
+            r.relay_out[i] = blocks[r.table[SEND + DIRECT * PLANES + b, lax.rem(col + k, COLS)]]
             return carry
 
         lax.fori_loop(0, OWNERS, fill, 0)
@@ -209,7 +211,7 @@
         for k in (4, 3, 5, 2, 6, 1, 7, 0):
             b = lax.rem(plane + k, PLANES)
             for e in range(extra):
-                block = r.relay_in[r.table[RELAY + b * max(EXTRAS) + e]]
+                block = r.relay_in[r.table[RELAY + e * PLANES + b, col]]
                 if k == 0:
                     landing[DIRECT * OWNERS + e] = block
                 else:
@@ -234,7 +236,7 @@
         def part(q):
             rows_of = [
                 jnp.concatenate(
-                    [landing[r.table[LAND + q * REQ + m * DOM + t]] for t in range(DOM)], axis=1
+                    [landing[r.table[LAND + m * DOM + t, col * PAIRS + q]] for t in range(DOM)], axis=1
                 )
                 for m in range(2)
             ]
@@ -417,10 +419,21 @@
     )(*([table, count, occ, source] + [coef] * exchanging + [energy, near, coupling, inter]))
 
 
-def padded_exchange(blocks, coef, send_pos, own_source, own_rank):
+def padded_exchange(blocks, coef, source_dev, block_pos, me):
+    source = source_dev.reshape(OWNERS, TOTAL)
+    position = block_pos.reshape(OWNERS, TOTAL)
+    wanted = source == me
+    ranking = jnp.cumsum(wanted.astype(jnp.int32), axis=1) - 1
+    slots = jnp.arange(CAP, dtype=jnp.int32)
+    chosen = wanted[:, None, :] & (ranking[:, None, :] == slots[None, :, None])
+    send_pos = jnp.sum(jnp.where(chosen, position[:, None, :], 0), axis=2)
     incoming = lax.all_to_all(
         blocks[send_pos], "pair", split_axis=0, concat_axis=0, tiled=True
     )
+    own_source = lax.dynamic_index_in_dim(source, me, 0, keepdims=False)
+    order = jnp.arange(TOTAL, dtype=jnp.int32)
+    earlier = (own_source[None, :] == own_source[:, None]) & (order[None, :] < order[:, None])
+    own_rank = jnp.sum(earlier.astype(jnp.int32), axis=1)
     arrived = incoming.reshape((OWNERS * CAP,) + blocks.shape[1:])[own_source * CAP + own_rank]
     arrived = arrived.reshape((PAIRS, 2, DOM) + blocks.shape[1:])
     coefs = coef.reshape(PAIRS, DOM, TILE, TILE)
@@ -432,52 +445,116 @@
     )
 
 
-def route(source_dev, block_pos, me):
+def route_kernel(source, position, table, most, by_tile, taken):
+    me = lax.axis_index("pair")
     plane, col = me // COLS, me % COLS
-    both = (source_dev * BLOCKS + block_pos).reshape(OWNERS, TOTAL)
-    source, position = both // BLOCKS, both % BLOCKS
-    slots = jnp.arange(CAP, dtype=jnp.int32)
-    devices = jnp.arange(OWNERS, dtype=jnp.int32)
-    wanted = source == me
-    ranking = jnp.cumsum(wanted.astype(jnp.int32), axis=1) - 1
-    chosen = wanted[:, None, :] & (ranking[:, None, :] == slots[None, :, None])
-    send_pos = jnp.sum(jnp.where(chosen, position[:, None, :], 0), axis=2)
-    taken = jnp.sum((source[:, None, :] == devices[None, :, None]).astype(jnp.int32), axis=2)
-    third = (taken > DIRECT).astype(jnp.int32)
-    most = jnp.max(jnp.sum(third.reshape(OWNERS, PLANES, COLS), axis=2))
-    room = jnp.minimum(jnp.maximum(most, EXTRAS[0]), EXTRAS[1])
-    own_source = lax.dynamic_index_in_dim(source, me, 0, keepdims=False)
-    order = jnp.arange(TOTAL, dtype=jnp.int32)
-    earlier = (own_source[None, :] == own_source[:, None]) & (order[None, :] < order[:, None])
-    own_rank = jnp.sum(earlier.astype(jnp.int32), axis=1)
-    own_third = lax.dynamic_index_in_dim(third, me, 0, keepdims=False)
-    before = (devices[None, :] < own_source[:, None]) & (
-        devices[None, :] // COLS == own_source[:, None] // COLS
+    lanes = PAIRS * COLS
+    for c in range(REQ):
+        for j in range(PLANES):
+            cut = slice(j * lanes, (j + 1) * lanes)
+            by_tile[0, c, j : j + 1, :] = source[c : c + 1, cut]
+            by_tile[1, c, j : j + 1, :] = position[c : c + 1, cut]
+    row = lax.broadcasted_iota(jnp.int32, (lanes, lanes), 0)
+    lane = lax.broadcasted_iota(jnp.int32, (lanes, lanes), 1)
+    earlier = ((row // PAIRS == lane // PAIRS) & (row < lane)).astype(jnp.float32)
+    device = (row // PAIRS == lane).astype(jnp.float32)
+
+    wanted = jnp.zeros((PLANES, lanes), jnp.float32)
+    where = jnp.zeros((PLANES, lanes), jnp.float32)
+    for c in range(REQ):
+        hit = by_tile[0, c] == me
+        wanted = wanted + jnp.where(hit, 1.0, 0.0)
+        where = where + jnp.where(hit, by_tile[1, c].astype(jnp.float32), 0.0)
+    rank = jnp.dot(wanted, earlier, preferred_element_type=jnp.float32)
+    for s in range(CAP):
+        chosen = jnp.where(rank == s, where, 0.0)
+        table[SEND + s * PLANES : SEND + (s + 1) * PLANES, :] = jnp.dot(
+            chosen, device, preferred_element_type=jnp.float32
+        ).astype(jnp.int32)
+
+    for s in range(OWNERS):
+        count = jnp.zeros((PLANES, lanes), jnp.float32)
+        for c in range(REQ):
+            count = count + jnp.where(by_tile[0, c] == s, 1.0, 0.0)
+        taken[s] = count
+    counts = jnp.dot(
+        taken[...].reshape(OWNERS * PLANES, lanes), device, preferred_element_type=jnp.float32
     )
-    extra_rank = jnp.sum(jnp.where(before, own_third[None, :], 0), axis=1)
+    taken[...] = jnp.where(counts > DIRECT, 1.0, 0.0).reshape(OWNERS, PLANES, lanes)
+    worst = jnp.zeros((PLANES, lanes), jnp.float32)
+    for a in range(PLANES):
+        total = taken[a * COLS]
+        for k in range(1, COLS):
+            total = total + taken[a * COLS + k]
+        worst = jnp.maximum(worst, total)
+    worst = jnp.max(worst).astype(jnp.int32)
+    most[0] = worst
+
+    planes = lax.broadcasted_iota(jnp.int32, (PLANES, lanes), 0)
+    before = jnp.zeros((PLANES, lanes), jnp.float32)
+    picked = [jnp.zeros((PLANES, lanes), jnp.int32) for _ in range(max(EXTRAS))]
+    for k in range(COLS):
+        third = taken[plane * COLS + k]
+        back = lax.rem(k - col + COLS, COLS)
+        for e in range(max(EXTRAS)):
+            picked[e] = picked[e] + jnp.where((third > 0.0) & (before == e), back, 0)
+        before = before + third
+    for e in range(max(EXTRAS)):
+        first = RELAY + e * PLANES
+        table[first : first + PLANES, :] = picked[e] * PLANES + planes
+
+    mine = source[:, pl.ds(pl.multiple_of(plane * lanes, lanes), lanes)]
+    place = lax.broadcasted_iota(jnp.int32, (REQ, lanes), 1) % PAIRS
+
+    def others(values, shift):
+        if shift:
+            inside = (place >= shift) & (place < PAIRS + shift)
+            values = jnp.where(inside, pltpu.roll(values, shift % lanes, 1), -1)
+        return [values] + [pltpu.roll(values, k, 0) for k in range(1, REQ)]
+
+    own_rank = jnp.zeros((REQ, lanes), jnp.int32)
+    for shift in range(1, PAIRS):
+        for other in others(mine, shift):
+            own_rank = own_rank + jnp.where(other == mine, 1, 0)
+    thirds = jnp.where(own_rank >= DIRECT, mine, -1)
+    first_of_plane = mine - mine % COLS
+    extra_rank = jnp.zeros((REQ, lanes), jnp.int32)
+    for shift in range(1 - PAIRS, PAIRS):
+        for other in others(thirds, shift):
+            extra_rank = extra_rank + jnp.where((other >= first_of_plane) & (other < mine), 1, 0)
+    room = jnp.clip(worst, EXTRAS[0], EXTRAS[1])
     extra_row = (
         DIRECT * OWNERS
-        + lax.rem(own_source // COLS - plane + PLANES, PLANES) * room
+        + ((mine // COLS - plane + PLANES) % PLANES) * room
         + jnp.minimum(extra_rank, room - 1)
     )
-    direct_row = lax.rem(own_source - me + OWNERS, OWNERS) * DIRECT + own_rank
-    land_row = jnp.where(own_rank >= DIRECT, extra_row, direct_row)
-    column = lax.dynamic_index_in_dim(third.reshape(PLANES, COLS, PLANES, COLS), col, 1, keepdims=False)
-    column = lax.dynamic_index_in_dim(column, plane, 1, keepdims=False)
-    cols = jnp.arange(COLS, dtype=jnp.int32)
-    place = jnp.cumsum(column, axis=1) - column
-    hit = (column == 1)[:, None, :] & (place[:, None, :] == jnp.arange(EXTRAS[1])[None, :, None])
-    back = lax.rem(cols - col + COLS, COLS)
-    relay_row = jnp.sum(jnp.where(hit, back[None, None, :], 0), axis=2) * PLANES + cols[:, None]
-    return send_pos, relay_row, land_row, own_source, own_rank, most
+    direct_row = ((mine - me + OWNERS) % OWNERS) * DIRECT + own_rank
+    table[LAND : LAND + REQ, :] = jnp.where(own_rank >= DIRECT, extra_row, direct_row)
+
+
+def route(source_dev, block_pos):
+    vmem = pl.BlockSpec(memory_space=pltpu.VMEM)
+    lanes = PAIRS * COLS
+    return pl.pallas_call(
+        route_kernel,
+        out_shape=(
+            jax.ShapeDtypeStruct((ROWS, lanes), jnp.int32),
+            jax.ShapeDtypeStruct((1,), jnp.int32),
+        ),
+        in_specs=[vmem, vmem],
+        out_specs=(vmem, pl.BlockSpec(memory_space=pltpu.SMEM)),
+        scratch_shapes=[
+            pltpu.VMEM((2, REQ, PLANES, lanes), jnp.int32),
+            pltpu.VMEM((OWNERS, PLANES, lanes), jnp.float32),
+        ],
+    )(source_dev.T, block_pos.T)
 
 
 def shards(
     blocks, pno_coef, source_dev, block_pos, pno_energy, occ_energy, pno_count, neighbour, coupling, intersection,
 ):
     me = lax.axis_index("pair")
-    send_pos, relay_row, land_row, own_source, own_rank, most = route(source_dev, block_pos, me)
-    table = jnp.concatenate([a.reshape(-1) for a in (send_pos, relay_row, land_row)])
+    table, most = route(source_dev, block_pos)
 
     def finish(extra, source):
         return run_kernel(
@@ -485,11 +562,11 @@
         )
 
     return lax.switch(
-        jnp.clip(most, 1, 3) - 1,
+        jnp.clip(most[0], 1, 3) - 1,
         [
             lambda: finish(1, blocks),
             lambda: finish(2, blocks),
-            lambda: finish(0, padded_exchange(blocks, pno_coef, send_pos, own_source, own_rank)),
+            lambda: finish(0, padded_exchange(blocks, pno_coef, source_dev, block_pos, me)),
         ],
     )
 

time: 167 us -> 164 us (0.982)
  other arithmetic: 3.81 us -> 0 us
  Pallas kernels: 156 us -> 158 us
    pallas_call x0 -> x1, Pallas kernels: none -> 2.03 us  [route(): pl.pallas_call(route_kernel, out_shape=(jax.ShapeDtypeStruct((ROWS, lanes...]
    reduce_sum x6 -> x0, other arithmetic: 1.74 us -> none  [the longest x1 1.15 us: route(): jnp.sum((source[:, None, :] == devices[None, :, None]).astype(jnp.int32),...]
where the time goes in v5:
time: 164 us; the launch traced here: 161 us
  Pallas kernels  158 us (96%)
    pallas_call x1, Pallas kernels, run_kernel(): pl.pallas_call(functools.partial(kernel, extra), out_shape=(jax.ShapeDtyp...  156 us

profile of v5, /device:TPU:25, one launch (start us, length us, event | category | flops | bytes accessed | tf_op | source)
XLA Modules:
  0.0 161.2 jit_solution(8757673682013446313)
XLA Ops:
  0.6 2.0 %shard_map.119 = (s32[48,128]{1,0:T(8,128)S(1)}, s32[1]{0:T(128)}) custom-call(s32[8,1024]{1,0:T(8,128)} %bitcast.45, s32[8,1024]{1,0:T(8,128)} %bitcast.46), custom_call_target="tpu_custom_call" | custom-call | tf_op jit(solution)/shard_map/pallas_call | solution.py:538
  3.3 156.4 %conditional.1 = ((f32[16,128,128]{2,1,0:T(8,128)S(1)}, f32[16]{0:T(128)S(1)})) conditional(s32[]{:T(128)} %bitcast.23, (s32[16,4]{0,1:T(4,128)}, f32[16,4]{0,1:T(4,128)}, s32[48,128]{1,0:T(8,128)S(1)}, s32[16]{0:T(128)}, f32[16]{0:T(128)}, /*index=5*/bf16[64,128,128]{2,1,0:T(8,128)(2,1)}, bf16[16,512,128]{2,1,0:T(8,128)(2,1)}, ...), branch_computations={%region_0.1_spmd, %region_1.2_spmd, %region_2.6_spmd} | conditional | flops 605752192 | bytes 83433528 | solution.py:564
  3.3 156.2 %branch_0_fun.1 = (f32[16,128,128]{2,1,0:T(8,128)S(1)}, f32[16]{0:T(128)S(1)}) custom-call(s32[48,128]{1,0:T(8,128)S(1)} %get-tuple-element.60.refs_0_, s32[16]{0:T(128)} %get-tuple-element.61.refs_1_, f32[16]{0:T(128)} %get-tuple-element.62.refs_2_, bf16[64,128,128]{2,1,0:T(8,128)(2,1)} %get-tuple-element.63.refs_3_, ...), custom_call_target="tpu_custom_call" | custom-call | tf_op jit(solution)/shard_map/cond/branch_0_fun/pallas_call | solution.py:405
  159.8 1.0 copy.38
  160.7 0.5 copy.39

commit v6 on v5

--- a/solution.py
+++ b/solution.py
@@ -308,7 +308,7 @@
             done.wait_send()
             done.wait_recv()
 
-    for k in (2, 1, 3):
+    for k in (1, 3, 2):
         for i in range(CHUNK):
             r.share_out[k - 1, i] = part(peers[k] * CHUNK + i).astype(jnp.bfloat16)
         share(k).start()
@@ -326,8 +326,8 @@
         r.low[own + i] = (values - top.astype(jnp.float32)).astype(jnp.bfloat16)
         return carry
 
-    lax.fori_loop(0, CHUNK, add, 0)
-    for k in (2, 1, 3):
+    lax.fori_loop(0, CHUNK, add, 0, unroll=True)
+    for k in (1, 3, 2):
         spread(HIGH, k).start()
 
     def first_amplitudes(start):
@@ -336,7 +336,7 @@
             windows[0][PAIRS + q] = (-r.high[q].astype(jnp.float32) * r.inverse[q]).astype(jnp.bfloat16)
             return carry
 
-        lax.fori_loop(0, CHUNK, body, 0)
+        lax.fori_loop(0, CHUNK, body, 0, unroll=True)
         for side in range(2):
             halo(0, start, CHUNK, side).start()
 
@@ -357,7 +357,7 @@
         if sweep == ITERS - 1:
             for k in (1, 3, 2):
                 wait_spread(LOW, k)
-            lax.fori_loop(0, PAIRS, both_halves, 0)
+            lax.fori_loop(0, PAIRS, both_halves, 0, unroll=CHUNK)
         wait_halo(sweep)
 
         def update(q, sweep=sweep):
@@ -381,15 +381,17 @@
                 r.amp[q] = current
                 r.pair_energy[q] = jnp.sum(r.factor[q] * current)
 
-        def some(j, carry, sweep=sweep):
-            for i in range(CHUNK):
-                update(j * CHUNK + i)
+        group = CHUNK if sweep < ITERS - 1 else 2 * CHUNK
+
+        def some(j, carry, sweep=sweep, group=group):
+            for i in range(group):
+                update(j * group + i)
             if sweep < ITERS - 1:
                 for side in range(2):
                     halo(sweep + 1, pl.multiple_of(j * CHUNK, CHUNK), CHUNK, side).start()
             return carry
 
-        lax.fori_loop(0, PAIRS // CHUNK, some, 0)
+        lax.fori_loop(0, PAIRS // group, some, 0)
 
     for k in range(1, AUXES):
         share(k).wait_send()

time: 164 us -> 163 us (level); the launches traced: 161 us -> 166 us
  Pallas kernels: 158 us -> 163 us
    pallas_call x1, Pallas kernels: 156 us -> 161 us  [run_kernel(): pl.pallas_call(functools.partial(kernel, extra), out_shape=(jax.ShapeDtyp...]
where the time goes in v6:
time: 163 us; the launch traced here: 166 us
  Pallas kernels  163 us (100%)
    pallas_call x1, Pallas kernels, run_kernel(): pl.pallas_call(functools.partial(kernel, extra), out_shape=(jax.ShapeDtyp...  161 us

profile of v6, /device:TPU:25, one launch (start us, length us, event | category | flops | bytes accessed | tf_op | source)
XLA Modules:
  0.0 166.5 jit_solution(6146615814124160906)
XLA Ops:
  0.6 2.0 %shard_map.119 = (s32[48,128]{1,0:T(8,128)S(1)}, s32[1]{0:T(128)}) custom-call(s32[8,1024]{1,0:T(8,128)} %bitcast.45, s32[8,1024]{1,0:T(8,128)} %bitcast.46), custom_call_target="tpu_custom_call" | custom-call | tf_op jit(solution)/shard_map/pallas_call | solution.py:540
  3.3 161.7 %conditional.1 = ((f32[16,128,128]{2,1,0:T(8,128)S(1)}, f32[16]{0:T(128)S(1)})) conditional(s32[]{:T(128)} %bitcast.23, (s32[16,4]{0,1:T(4,128)}, f32[16,4]{0,1:T(4,128)}, s32[48,128]{1,0:T(8,128)S(1)}, s32[16]{0:T(128)}, f32[16]{0:T(128)}, /*index=5*/bf16[64,128,128]{2,1,0:T(8,128)(2,1)}, bf16[16,512,128]{2,1,0:T(8,128)(2,1)}, ...), branch_computations={%region_0.1_spmd, %region_1.2_spmd, %region_2.6_spmd} | conditional | flops 605752192 | bytes 83433528 | solution.py:566
  3.5 161.2 %branch_1_fun.1 = (f32[16,128,128]{2,1,0:T(8,128)S(1)}, f32[16]{0:T(128)S(1)}) custom-call(s32[48,128]{1,0:T(8,128)S(1)} %get-tuple-element.69.refs_0_, s32[16]{0:T(128)} %get-tuple-element.70.refs_1_, f32[16]{0:T(128)} %get-tuple-element.71.refs_2_, bf16[64,128,128]{2,1,0:T(8,128)(2,1)} %get-tuple-element.72.refs_3_, ...), custom_call_target="tpu_custom_call" | custom-call | tf_op jit(solution)/shard_map/cond/branch_1_fun/pallas_call | solution.py:407
  165.0 1.0 copy.38
  166.0 0.5 copy.39
